TPU v7x, 32 devices: a whole 2x2x4 slice. The times are simulated.
32 devices in a mesh: cols: 8 (over z, x), par: 4 (over y, core).
Axes of the slice: x: 2, y: 2, z: 4, core: 2. Of those that a mesh axis runs over, the one named last changes fastest.
Arguments:
- tile_bounds: int32 [9], replicated, may hold values from 0 to 2048, as said below
- tile_anchor: int32 [64, 2], P(('cols', 'par')), may hold values from 0 to 256, as said below
- tile_picks: int32 [64], P(('cols', 'par')), may hold values from 16 to 64, as said below
- rmo_picks: bfloat16 [64, 64], P(('cols', 'par')), may hold values from -6 to 6
- sensitivity: bfloat16 [64, 64, 3, 16, 128], P(('cols', 'par')), may hold values from -0.75 to 0.75
- dip_class: int32 [32, 8, 256], P(('cols', 'par')), may hold values from 0 to 8
- strength: float32 [3], replicated, may hold values from 0.05 to 0.2
- couple: float32 [3, 3], replicated, may hold values from 0.1 to 1
Outputs:
- model_update: float32 [3, 32, 8, 256], P(None, ('cols', 'par'))
Inputs may be any that keep to these rules, and one draw needn't show every extreme that they name: tile_bounds[0] = 0 and tile_bounds[8] = 2048; column tile c holds grid columns tile_bounds[c] to tile_bounds[c + 1] - 1, between 128 and 384 of them, and some column tile holds exactly 384. Fat-ray tile t belongs to column tile t // (2 * 4); it covers depth cells tile_anchor[t, 0] to tile_anchor[t, 0] + 15 and column slots tile_anchor[t, 1] to tile_anchor[t, 1] + 127 of that column tile, all of them among its columns and within the grid. Rays 0 to tile_picks[t] - 1 of tile t are live; some tile has 64 live rays.
All inputs are finite; a program needn't handle non-finite values.
Results may differ from a plain program's by a relative error of at most 0.0003.
Values sent between devices are 32-bit elements; how exact they have to be, the bound alone decides.
No kernel may reach another device: no remote copies, remote signals or barrier semaphores. Data moves between devices by JAX's collectives and lax.ppermute only.
A program may use at most 192 MiB of HBM per device.

v0:
```python
import jax
import jax.numpy as jnp
from jax import lax
from jax.sharding import PartitionSpec as P

CAP = 384
PASSES = 6


def extended(block, sides, width):
    for axis, dim in sides:
        count = lax.axis_size(axis)
        forward = [(i, i + 1) for i in range(count - 1)]
        backward = [(target, source) for source, target in forward]
        low = lax.ppermute(
            lax.slice_in_dim(block, block.shape[dim] - width, None, axis=dim), axis, forward
        )
        high = lax.ppermute(lax.slice_in_dim(block, 0, width, axis=dim), axis, backward)
        block = jnp.concatenate([low, block, high], axis=dim)
    return block


def next_cells(values, along_dim):
    count = values.shape[along_dim]
    kept = lax.slice_in_dim(values, 1, count, axis=along_dim)
    zeros = jnp.zeros_like(lax.slice_in_dim(values, 0, 1, axis=along_dim))
    return jnp.concatenate([kept, zeros], axis=along_dim)


def prev_cells(values, along_dim):
    count = values.shape[along_dim]
    kept = lax.slice_in_dim(values, 0, count - 1, axis=along_dim)
    zeros = jnp.zeros_like(lax.slice_in_dim(values, 0, 1, axis=along_dim))
    return jnp.concatenate([zeros, kept], axis=along_dim)


def at_depth(padded, tilt):
    return jnp.where(tilt < 0, padded[:, :-2], jnp.where(tilt > 0, padded[:, 2:], padded[:, 1:-1]))


def smooth_pass(padded, dip_class, strength, mixing):
    centre = padded[:, 1:-1]
    tilt_across = (dip_class // 3 - 1)[None]
    tilt_along = (dip_class % 3 - 1)[None]
    east_side = at_depth(next_cells(padded, 2), tilt_across)
    west_side = at_depth(prev_cells(padded, 2), -tilt_across)
    north_side = at_depth(next_cells(padded, 3), tilt_along)
    south_side = at_depth(prev_cells(padded, 3), -tilt_along)
    laplace = east_side + west_side + north_side + south_side - 4.0 * centre
    smooth = centre + strength[:, None, None, None] * laplace
    return jnp.tensordot(mixing, smooth, axes=1, precision=lax.Precision.HIGHEST)


def shards(
    tile_bounds, tile_anchor, tile_picks, rmo_picks, sensitivity, dip_class, strength, couple
):
    tile_count, ray_count, param_count, depth_cells, tile_columns = sensitivity.shape
    col_devices = lax.axis_size("cols")
    par_devices = lax.axis_size("par")
    slab_depth, rows_x, rows_y = dip_class.shape
    total_depth = slab_depth * col_devices * par_devices
    live = jnp.arange(ray_count, dtype=jnp.int32)[None, :] < tile_picks[:, None]
    ray_weight = jnp.where(live, rmo_picks, jnp.zeros_like(rmo_picks))
    contribution = jnp.einsum(
        "tr,trk->tk",
        ray_weight,
        sensitivity.reshape(tile_count, ray_count, -1),
        preferred_element_type=jnp.float32,
    )
    contribution = contribution.reshape(tile_count, param_count, depth_cells, tile_columns)

    def add_tile(tile_number, gradient):
        anchor = (jnp.int32(0), tile_anchor[tile_number, 0], tile_anchor[tile_number, 1])
        current = lax.dynamic_slice(gradient, anchor, (param_count, depth_cells, tile_columns))
        return lax.dynamic_update_slice(gradient, current + contribution[tile_number], anchor)

    gradient = jnp.zeros((param_count, total_depth, CAP), jnp.float32)
    gradient = lax.fori_loop(0, tile_count, add_tile, gradient)
    blocks = gradient.reshape(param_count, col_devices, par_devices, slab_depth, CAP)
    reduced = lax.psum_scatter(blocks, "par", scatter_dimension=2, tiled=True)
    summed = lax.all_to_all(reduced, "cols", split_axis=1, concat_axis=4, tiled=True)
    padded_slots = summed.reshape(param_count, slab_depth, col_devices * CAP)
    columns = rows_x * rows_y
    column_ids = jnp.arange(columns, dtype=jnp.int32)
    starts = tile_bounds[:-1]
    below = starts[None, :] <= column_ids[:, None]
    owner_tile = jnp.sum(below.astype(jnp.int32), axis=1) - 1
    tile_start = jnp.max(jnp.where(below, starts[None, :], jnp.zeros_like(starts)[None, :]), axis=1)
    slot_index = owner_tile * CAP + column_ids - tile_start
    field = jnp.take(padded_slots, slot_index, axis=2).reshape(
        param_count, slab_depth, rows_x, rows_y
    )
    mixing = couple / jnp.sum(couple, axis=1, keepdims=True)
    for _ in range(PASSES):
        padded = extended(field, ((("cols", "par"), 1),), 1)
        field = smooth_pass(padded, dip_class, strength, mixing)
    return field


def solution(mesh):
    return jax.shard_map(
        shards,
        mesh=mesh,
        in_specs=(
            P(),
            P(("cols", "par"), None),
            P(("cols", "par")),
            P(("cols", "par"), None),
            P(("cols", "par"), None, None, None, None),
            P(("cols", "par"), None, None),
            P(),
            P(),
        ),
        out_specs=P(None, ("cols", "par"), None, None),
        check_vma=False,
    )
```

profile of v0, /device:TPU:7, one launch (start us, length us, event | category | flops | bytes accessed | tf_op | source)
XLA Modules:
  0.0 128.5 jit_solution(18314591592560090305)
XLA Ops:
  6.5 2.5 %reshape.228 = bf16[2,64,6144]{2,1,0:T(8,128)(2,1)S(1)} reshape(bf16[2,64,3,16,128]{4,3,2,1,0:T(8,128)(2,1)} %param.14) | data formatting | bytes 3145728 | tf_op jit(solution)/shard_map/reshape | solution.py:67
  9.2 0.3 fusion.170
  9.6 0.2 copy-done
  9.8 12.0 %while.13 = (s32[]{:T(128)}, f32[3,32,384]{2,1,0:T(8,128)S(1)}, s32[2,2]{1,0:T(2,128)S(1)}, f32[2,3,16,128]{3,2,1,0:T(8,128)S(1)}, s32[]{:T(128)}, /*index=5*/s32[]{:T(128)}, s32[]{:T(128)}, s32[]{:T(128)}) while((s32[]{:T(128)}, f32[3,32,384]{2,1,0:T(8,128)S(1)}, s32[2,2]{1,0:T(2,128)S(1)}, f32[2,3,16,128]{3,2,1,0:T(8,128)S(1)}, s32[]{:T(128)}, ...), condition=%wide.region_4.5_spmd, body=%wide.region_3.4_spmd.sunk | while | flops 6152 | bytes 123069 | solution.py:78
  9.8 0.6 constant_dynamic-slice_fusion.3
  14.2 1.6 %dynamic_update_slice.8 = f32[3,32,384]{2,1,0:T(8,128)S(1)} dynamic-update-slice(f32[3,32,384]{2,1,0:T(8,128)S(1)} %get-tuple-element.168, f32[3,16,128]{2,1,0:T(8,128)S(1)} %bitcast_add_fusion.2, s32[]{:T(128)} %constant.105.clone.1..sunk, s32[]{:T(128)S(6)} %select_n.667, s32[]{:T(128)S(6)} %select_n.668) | dynamic-update-slice | bytes 49156 | tf_op jit(solution)/shard_map/while/body/eval_jaxpr/dynamic_update_slice | solution.py:75
  15.8 0.6 constant_dynamic-slice_fusion.3
  20.2 1.6 %dynamic_update_slice.8 = f32[3,32,384]{2,1,0:T(8,128)S(1)} dynamic-update-slice(f32[3,32,384]{2,1,0:T(8,128)S(1)} %get-tuple-element.168, f32[3,16,128]{2,1,0:T(8,128)S(1)} %bitcast_add_fusion.2, s32[]{:T(128)} %constant.105.clone.1..sunk, s32[]{:T(128)S(6)} %select_n.667, s32[]{:T(128)S(6)} %select_n.668) | dynamic-update-slice | bytes 49156 | tf_op jit(solution)/shard_map/while/body/eval_jaxpr/dynamic_update_slice | solution.py:75
  21.9 0.7 copy.30
  22.6 0.1 convert_reduce_fusion
  22.8 19.4 %reduce-scatter.4.cloned.1.call-done = f32[3,8,1,1,384]{4,1,3,0,2:T(8,128)} async-done(((f32[3,8,4,1,384]{4,1,3,0,2:T(8,128)}), f32[3,8,1,1,384]{4,1,3,0,2:T(8,128)}) %reduce-scatter.4.cloned.1.call-update) | async-done | bytes 36880
  42.2 1.4 %copy.31 = f32[3,8,1,1,384]{4,3,2,0,1:T(1,128)} copy(f32[3,8,1,1,384]{4,1,3,0,2:T(8,128)} %reduce-scatter.4.cloned.1.call-done) | data formatting | bytes 73728 | tf_op jit(solution)/shard_map/reduce_scatter | solution.py:80
  43.6 5.6 %all-to-all-start = ((f32[3,8,1,1,384]{4,3,2,0,1:T(1,128)}), f32[3,8,1,1,384]{4,3,2,0,1:T(1,128)S(1)}, u32[]{:S(2)}, u32[]{:S(2)}) async-start(f32[3,8,1,1,384]{4,3,2,0,1:T(1,128)} %copy.31), calls=%async_computation | async-start | bytes 73728 | tf_op jit(solution)/shard_map/all_to_all | solution.py:81
  49.3 4.4 %all-to-all-done = f32[3,8,1,1,384]{4,3,2,0,1:T(1,128)S(1)} async-done(((f32[3,8,1,1,384]{4,3,2,0,1:T(1,128)}), f32[3,8,1,1,384]{4,3,2,0,1:T(1,128)S(1)}, u32[]{:S(2)}, u32[]{:S(2)}) %all-to-all-start) | async-done | bytes 36896 | tf_op jit(solution)/shard_map/all_to_all | solution.py:81
  53.6 0.5 copy.32
  54.1 5.5 %gather_fusion = f32[2048,3]{1,0:T(8,128)S(1)} fusion(f32[3,3072]{0,1:T(8,128)S(1)} %bitcast.129, s32[2048]{0:T(1024)S(1)} %broadcast_clamp_fusion), kind=kCustom, calls=%fused_computation | custom fusion | bytes 57344 | tf_op jit(solution)/shard_map/jit(_take)/gather | solution.py:90
  59.6 0.3 copy.34
  60.0 6.3 %collective-permute-start = (f32[3,1,8,256]{3,0,2,1:T(4,128)S(1)}, f32[3,1,8,256]{3,0,2,1:T(4,128)S(1)}, u32[]{:S(2)}, u32[]{:S(2)}) collective-permute-start(f32[3,1,8,256]{3,0,2,1:T(4,128)S(1)} %broadcast_select_fusion), channel_id=1, source_target_pairs={{0,1},{1,2},{2,3},{3,4},{4,5},{5,6},{6,7},{7,8},{8,9},{9,10},{10,1... | collective-permute-start | bytes 73736 | tf_op jit(solution)/shard_map/ppermute | solution.py:15
  66.3 1.9 %collective-permute-start.1 = (f32[3,1,8,256]{3,0,2,1:T(4,128)S(1)}, f32[3,1,8,256]{3,0,2,1:T(4,128)S(1)}, u32[]{:S(2)}, u32[]{:S(2)}) collective-permute-start(f32[3,1,8,256]{3,0,2,1:T(4,128)S(1)} %broadcast_select_fusion), channel_id=1, source_target_pairs={{1,0},{2,1},{3,2},{4,3},{5,4},{6,5},{7,6},{8,7},{9,8},{10,9},{11,1... | collective-permute-start | bytes 73736 | tf_op jit(solution)/shard_map/ppermute | solution.py:18
  68.2 0.1 reduce_sum.18
  68.3 5.0 %collective-permute-done.1 = f32[3,1,8,256]{3,0,2,1:T(4,128)S(1)} collective-permute-done((f32[3,1,8,256]{3,0,2,1:T(4,128)S(1)}, f32[3,1,8,256]{3,0,2,1:T(4,128)S(1)}, u32[]{:S(2)}, u32[]{:S(2)}) %collective-permute-start.1) | collective-permute-done | bytes 24608 | tf_op jit(solution)/shard_map/ppermute | solution.py:18
  73.3 0.1 fusion.202
  73.5 0.3 fusion.93
  73.8 1.9 %collective-permute-start.2 = (f32[3,1,8,256]{3,0,2,1:T(4,128)S(1)}, f32[3,1,8,256]{3,0,2,1:T(4,128)S(1)}, u32[]{:S(2)}, u32[]{:S(2)}) collective-permute-start(f32[3,1,8,256]{3,0,2,1:T(4,128)S(1)} %bitcast.139), channel_id=1, source_target_pairs={{0,1},{1,2},{2,3},{3,4},{4,5},{5,6},{6,7},{7,8},{8,9},{9,10},{10,1... | collective-permute-start | bytes 73736 | tf_op jit(solution)/shard_map/ppermute | solution.py:15
  75.7 2.4 %collective-permute-start.3 = (f32[3,1,8,256]{3,0,2,1:T(4,128)S(1)}, f32[3,1,8,256]{3,0,2,1:T(4,128)S(1)}, u32[]{:S(2)}, u32[]{:S(2)}) collective-permute-start(f32[3,1,8,256]{3,0,2,1:T(4,128)S(1)} %bitcast.140), channel_id=1, source_target_pairs={{1,0},{2,1},{3,2},{4,3},{5,4},{6,5},{7,6},{8,7},{9,8},{10,9},{11,1... | collective-permute-start | bytes 73736 | tf_op jit(solution)/shard_map/ppermute | solution.py:18
  78.1 4.6 %collective-permute-done.3 = f32[3,1,8,256]{3,0,2,1:T(4,128)S(1)} collective-permute-done((f32[3,1,8,256]{3,0,2,1:T(4,128)S(1)}, f32[3,1,8,256]{3,0,2,1:T(4,128)S(1)}, u32[]{:S(2)}, u32[]{:S(2)}) %collective-permute-start.3) | collective-permute-done | bytes 24608 | tf_op jit(solution)/shard_map/ppermute | solution.py:18
  82.8 0.1 fusion.200
  82.9 0.3 fusion.91
  83.3 1.9 %collective-permute-start.4 = (f32[3,1,8,256]{3,0,2,1:T(4,128)S(1)}, f32[3,1,8,256]{3,0,2,1:T(4,128)S(1)}, u32[]{:S(2)}, u32[]{:S(2)}) collective-permute-start(f32[3,1,8,256]{3,0,2,1:T(4,128)S(1)} %bitcast.142), channel_id=1, source_target_pairs={{0,1},{1,2},{2,3},{3,4},{4,5},{5,6},{6,7},{7,8},{8,9},{9,10},{10,1... | collective-permute-start | bytes 73736 | tf_op jit(solution)/shard_map/ppermute | solution.py:15
  85.2 2.4 %collective-permute-start.5 = (f32[3,1,8,256]{3,0,2,1:T(4,128)S(1)}, f32[3,1,8,256]{3,0,2,1:T(4,128)S(1)}, u32[]{:S(2)}, u32[]{:S(2)}) collective-permute-start(f32[3,1,8,256]{3,0,2,1:T(4,128)S(1)} %bitcast.143), channel_id=1, source_target_pairs={{1,0},{2,1},{3,2},{4,3},{5,4},{6,5},{7,6},{8,7},{9,8},{10,9},{11,1... | collective-permute-start | bytes 73736 | tf_op jit(solution)/shard_map/ppermute | solution.py:18
  87.6 4.6 %collective-permute-done.5 = f32[3,1,8,256]{3,0,2,1:T(4,128)S(1)} collective-permute-done((f32[3,1,8,256]{3,0,2,1:T(4,128)S(1)}, f32[3,1,8,256]{3,0,2,1:T(4,128)S(1)}, u32[]{:S(2)}, u32[]{:S(2)}) %collective-permute-start.5) | collective-permute-done | bytes 24608 | tf_op jit(solution)/shard_map/ppermute | solution.py:18
  92.2 0.1 fusion.198
  92.4 0.3 fusion.89
  92.7 1.9 %collective-permute-start.6 = (f32[3,1,8,256]{3,0,2,1:T(4,128)S(1)}, f32[3,1,8,256]{3,0,2,1:T(4,128)S(1)}, u32[]{:S(2)}, u32[]{:S(2)}) collective-permute-start(f32[3,1,8,256]{3,0,2,1:T(4,128)S(1)} %bitcast.145), channel_id=1, source_target_pairs={{0,1},{1,2},{2,3},{3,4},{4,5},{5,6},{6,7},{7,8},{8,9},{9,10},{10,1... | collective-permute-start | bytes 73736 | tf_op jit(solution)/shard_map/ppermute | solution.py:15
  94.6 2.4 %collective-permute-start.7 = (f32[3,1,8,256]{3,0,2,1:T(4,128)S(1)}, f32[3,1,8,256]{3,0,2,1:T(4,128)S(1)}, u32[]{:S(2)}, u32[]{:S(2)}) collective-permute-start(f32[3,1,8,256]{3,0,2,1:T(4,128)S(1)} %bitcast.146), channel_id=1, source_target_pairs={{1,0},{2,1},{3,2},{4,3},{5,4},{6,5},{7,6},{8,7},{9,8},{10,9},{11,1... | collective-permute-start | bytes 73736 | tf_op jit(solution)/shard_map/ppermute | solution.py:18
  97.1 4.6 %collective-permute-done.7 = f32[3,1,8,256]{3,0,2,1:T(4,128)S(1)} collective-permute-done((f32[3,1,8,256]{3,0,2,1:T(4,128)S(1)}, f32[3,1,8,256]{3,0,2,1:T(4,128)S(1)}, u32[]{:S(2)}, u32[]{:S(2)}) %collective-permute-start.7) | collective-permute-done | bytes 24608 | tf_op jit(solution)/shard_map/ppermute | solution.py:18
  101.7 0.1 fusion.196
  101.8 0.3 fusion.87
  102.2 1.9 %collective-permute-start.8 = (f32[3,1,8,256]{3,0,2,1:T(4,128)S(1)}, f32[3,1,8,256]{3,0,2,1:T(4,128)S(1)}, u32[]{:S(2)}, u32[]{:S(2)}) collective-permute-start(f32[3,1,8,256]{3,0,2,1:T(4,128)S(1)} %bitcast.148), channel_id=1, source_target_pairs={{0,1},{1,2},{2,3},{3,4},{4,5},{5,6},{6,7},{7,8},{8,9},{9,10},{10,1... | collective-permute-start | bytes 73736 | tf_op jit(solution)/shard_map/ppermute | solution.py:15
  104.1 2.4 %collective-permute-start.9 = (f32[3,1,8,256]{3,0,2,1:T(4,128)S(1)}, f32[3,1,8,256]{3,0,2,1:T(4,128)S(1)}, u32[]{:S(2)}, u32[]{:S(2)}) collective-permute-start(f32[3,1,8,256]{3,0,2,1:T(4,128)S(1)} %bitcast.149), channel_id=1, source_target_pairs={{1,0},{2,1},{3,2},{4,3},{5,4},{6,5},{7,6},{8,7},{9,8},{10,9},{11,1... | collective-permute-start | bytes 73736 | tf_op jit(solution)/shard_map/ppermute | solution.py:18
  106.5 4.6 %collective-permute-done.9 = f32[3,1,8,256]{3,0,2,1:T(4,128)S(1)} collective-permute-done((f32[3,1,8,256]{3,0,2,1:T(4,128)S(1)}, f32[3,1,8,256]{3,0,2,1:T(4,128)S(1)}, u32[]{:S(2)}, u32[]{:S(2)}) %collective-permute-start.9) | collective-permute-done | bytes 24608 | tf_op jit(solution)/shard_map/ppermute | solution.py:18
  111.3 0.3 fusion.85
  111.6 1.9 %collective-permute-start.10 = (f32[3,1,8,256]{3,0,2,1:T(4,128)S(1)}, f32[3,1,8,256]{3,0,2,1:T(4,128)S(1)}, u32[]{:S(2)}, u32[]{:S(2)}) collective-permute-start(f32[3,1,8,256]{3,0,2,1:T(4,128)S(1)} %bitcast.136), channel_id=1, source_target_pairs={{0,1},{1,2},{2,3},{3,4},{4,5},{5,6},{6,7},{7,8},{8,9},{9,10},{10,1... | collective-permute-start | bytes 73736 | tf_op jit(solution)/shard_map/ppermute | solution.py:15
  113.6 2.4 %collective-permute-start.11 = (f32[3,1,8,256]{3,0,2,1:T(4,128)S(1)}, f32[3,1,8,256]{3,0,2,1:T(4,128)S(1)}, u32[]{:S(2)}, u32[]{:S(2)}) collective-permute-start(f32[3,1,8,256]{3,0,2,1:T(4,128)S(1)} %bitcast.137), channel_id=1, source_target_pairs={{1,0},{2,1},{3,2},{4,3},{5,4},{6,5},{7,6},{8,7},{9,8},{10,9},{11,1... | collective-permute-start | bytes 73736 | tf_op jit(solution)/shard_map/ppermute | solution.py:18
  116.0 4.6 %collective-permute-done.11 = f32[3,1,8,256]{3,0,2,1:T(4,128)S(1)} collective-permute-done((f32[3,1,8,256]{3,0,2,1:T(4,128)S(1)}, f32[3,1,8,256]{3,0,2,1:T(4,128)S(1)}, u32[]{:S(2)}, u32[]{:S(2)}) %collective-permute-start.11) | collective-permute-done | bytes 24608 | tf_op jit(solution)/shard_map/ppermute | solution.py:18
  120.6 0.1 fusion.192
  120.8 0.3 convolution_bitcast_fusion
  121.1 0.6 copy.35
  (50 shorter events, 0.9 us)
Async XLA Ops:
  6.5 2.5 %copy-start.5 = (s32[2]{0:T(128)S(1)}, s32[2]{0:T(128)}, u32[]{:S(2)}) copy-start(s32[2]{0:T(128)} %param.12) | copy-start | bytes 28
  6.5 2.6 %copy-start.4 = (bf16[2,64]{1,0:T(2,128)(2,1)S(1)}, bf16[2,64]{1,0:T(2,128)(2,1)}, u32[]{:S(2)}) copy-start(bf16[2,64]{1,0:T(2,128)(2,1)} %param.13) | copy-start | bytes 772
  6.5 35.7 %reduce-scatter.4.cloned.1.call-start = ((), (), s32[]{:S(2)}) async-start(), calls=%async_computation.2 | async-start | bytes 184320
  9.1 0.7 copy-start
  9.2 13.4 %copy-start.3 = (s32[9]{0:T(128)S(1)}, s32[9]{0:T(128)}, u32[]{:S(2)}) copy-start(s32[9]{0:T(128)} %param.10) | copy-start | bytes 112
  9.2 13.6 %copy-start.1 = (s32[1,8,256]{2,1,0:T(8,128)S(1)}, s32[1,8,256]{2,1,0:T(8,128)}, u32[]{:S(2)}) copy-start(s32[1,8,256]{2,1,0:T(8,128)} %param.15) | copy-start | bytes 24580
  43.6 24.6 %copy-start.2 = (f32[3,3]{1,0:T(4,128)S(1)}, f32[3,3]{1,0:T(4,128)}, u32[]{:S(2)}) copy-start(f32[3,3]{1,0:T(4,128)} %param.17) | copy-start | bytes 112
  43.6 10.0 %all-to-all-start = ((f32[3,8,1,1,384]{4,3,2,0,1:T(1,128)}), f32[3,8,1,1,384]{4,3,2,0,1:T(1,128)S(1)}, u32[]{:S(2)}, u32[]{:S(2)}) async-start(f32[3,8,1,1,384]{4,3,2,0,1:T(1,128)} %copy.31), calls=%async_computation | async-start | bytes 73728 | tf_op jit(solution)/shard_map/all_to_all | solution.py:81
  54.1 19.3 %copy-start.6 = (f32[3]{0:T(128)S(1)}, f32[3]{0:T(128)}, u32[]{:S(2)}) copy-start(f32[3]{0:T(128)} %param.16) | copy-start | bytes 40
  60.0 8.4 %collective-permute-start = (f32[3,1,8,256]{3,0,2,1:T(4,128)S(1)}, f32[3,1,8,256]{3,0,2,1:T(4,128)S(1)}, u32[]{:S(2)}, u32[]{:S(2)}) collective-permute-start(f32[3,1,8,256]{3,0,2,1:T(4,128)S(1)} %broadcast_select_fusion), channel_id=1, source_target_pairs={{0,1},{1,2},{2,3},{3,4},{4,5},{5,6},{6,7},{7,8},{8,9},{9,10},{10,1... | collective-permute-start | bytes 73736 | tf_op jit(solution)/shard_map/ppermute | solution.py:15
  66.3 7.0 %collective-permute-start.1 = (f32[3,1,8,256]{3,0,2,1:T(4,128)S(1)}, f32[3,1,8,256]{3,0,2,1:T(4,128)S(1)}, u32[]{:S(2)}, u32[]{:S(2)}) collective-permute-start(f32[3,1,8,256]{3,0,2,1:T(4,128)S(1)} %broadcast_select_fusion), channel_id=1, source_target_pairs={{1,0},{2,1},{3,2},{4,3},{5,4},{6,5},{7,6},{8,7},{9,8},{10,9},{11,1... | collective-permute-start | bytes 73736 | tf_op jit(solution)/shard_map/ppermute | solution.py:18
  73.8 4.3 %collective-permute-start.2 = (f32[3,1,8,256]{3,0,2,1:T(4,128)S(1)}, f32[3,1,8,256]{3,0,2,1:T(4,128)S(1)}, u32[]{:S(2)}, u32[]{:S(2)}) collective-permute-start(f32[3,1,8,256]{3,0,2,1:T(4,128)S(1)} %bitcast.139), channel_id=1, source_target_pairs={{0,1},{1,2},{2,3},{3,4},{4,5},{5,6},{6,7},{7,8},{8,9},{9,10},{10,1... | collective-permute-start | bytes 73736 | tf_op jit(solution)/shard_map/ppermute | solution.py:15
  75.7 7.0 %collective-permute-start.3 = (f32[3,1,8,256]{3,0,2,1:T(4,128)S(1)}, f32[3,1,8,256]{3,0,2,1:T(4,128)S(1)}, u32[]{:S(2)}, u32[]{:S(2)}) collective-permute-start(f32[3,1,8,256]{3,0,2,1:T(4,128)S(1)} %bitcast.140), channel_id=1, source_target_pairs={{1,0},{2,1},{3,2},{4,3},{5,4},{6,5},{7,6},{8,7},{9,8},{10,9},{11,1... | collective-permute-start | bytes 73736 | tf_op jit(solution)/shard_map/ppermute | solution.py:18
  83.3 4.3 %collective-permute-start.4 = (f32[3,1,8,256]{3,0,2,1:T(4,128)S(1)}, f32[3,1,8,256]{3,0,2,1:T(4,128)S(1)}, u32[]{:S(2)}, u32[]{:S(2)}) collective-permute-start(f32[3,1,8,256]{3,0,2,1:T(4,128)S(1)} %bitcast.142), channel_id=1, source_target_pairs={{0,1},{1,2},{2,3},{3,4},{4,5},{5,6},{6,7},{7,8},{8,9},{9,10},{10,1... | collective-permute-start | bytes 73736 | tf_op jit(solution)/shard_map/ppermute | solution.py:15
  85.2 7.0 %collective-permute-start.5 = (f32[3,1,8,256]{3,0,2,1:T(4,128)S(1)}, f32[3,1,8,256]{3,0,2,1:T(4,128)S(1)}, u32[]{:S(2)}, u32[]{:S(2)}) collective-permute-start(f32[3,1,8,256]{3,0,2,1:T(4,128)S(1)} %bitcast.143), channel_id=1, source_target_pairs={{1,0},{2,1},{3,2},{4,3},{5,4},{6,5},{7,6},{8,7},{9,8},{10,9},{11,1... | collective-permute-start | bytes 73736 | tf_op jit(solution)/shard_map/ppermute | solution.py:18
  92.7 4.3 %collective-permute-start.6 = (f32[3,1,8,256]{3,0,2,1:T(4,128)S(1)}, f32[3,1,8,256]{3,0,2,1:T(4,128)S(1)}, u32[]{:S(2)}, u32[]{:S(2)}) collective-permute-start(f32[3,1,8,256]{3,0,2,1:T(4,128)S(1)} %bitcast.145), channel_id=1, source_target_pairs={{0,1},{1,2},{2,3},{3,4},{4,5},{5,6},{6,7},{7,8},{8,9},{9,10},{10,1... | collective-permute-start | bytes 73736 | tf_op jit(solution)/shard_map/ppermute | solution.py:15
  94.6 7.0 %collective-permute-start.7 = (f32[3,1,8,256]{3,0,2,1:T(4,128)S(1)}, f32[3,1,8,256]{3,0,2,1:T(4,128)S(1)}, u32[]{:S(2)}, u32[]{:S(2)}) collective-permute-start(f32[3,1,8,256]{3,0,2,1:T(4,128)S(1)} %bitcast.146), channel_id=1, source_target_pairs={{1,0},{2,1},{3,2},{4,3},{5,4},{6,5},{7,6},{8,7},{9,8},{10,9},{11,1... | collective-permute-start | bytes 73736 | tf_op jit(solution)/shard_map/ppermute | solution.py:18
  102.2 4.3 %collective-permute-start.8 = (f32[3,1,8,256]{3,0,2,1:T(4,128)S(1)}, f32[3,1,8,256]{3,0,2,1:T(4,128)S(1)}, u32[]{:S(2)}, u32[]{:S(2)}) collective-permute-start(f32[3,1,8,256]{3,0,2,1:T(4,128)S(1)} %bitcast.148), channel_id=1, source_target_pairs={{0,1},{1,2},{2,3},{3,4},{4,5},{5,6},{6,7},{7,8},{8,9},{9,10},{10,1... | collective-permute-start | bytes 73736 | tf_op jit(solution)/shard_map/ppermute | solution.py:15
  104.1 7.0 %collective-permute-start.9 = (f32[3,1,8,256]{3,0,2,1:T(4,128)S(1)}, f32[3,1,8,256]{3,0,2,1:T(4,128)S(1)}, u32[]{:S(2)}, u32[]{:S(2)}) collective-permute-start(f32[3,1,8,256]{3,0,2,1:T(4,128)S(1)} %bitcast.149), channel_id=1, source_target_pairs={{1,0},{2,1},{3,2},{4,3},{5,4},{6,5},{7,6},{8,7},{9,8},{10,9},{11,1... | collective-permute-start | bytes 73736 | tf_op jit(solution)/shard_map/ppermute | solution.py:18
  111.6 4.3 %collective-permute-start.10 = (f32[3,1,8,256]{3,0,2,1:T(4,128)S(1)}, f32[3,1,8,256]{3,0,2,1:T(4,128)S(1)}, u32[]{:S(2)}, u32[]{:S(2)}) collective-permute-start(f32[3,1,8,256]{3,0,2,1:T(4,128)S(1)} %bitcast.136), channel_id=1, source_target_pairs={{0,1},{1,2},{2,3},{3,4},{4,5},{5,6},{6,7},{7,8},{8,9},{9,10},{10,1... | collective-permute-start | bytes 73736 | tf_op jit(solution)/shard_map/ppermute | solution.py:15
  113.6 7.0 %collective-permute-start.11 = (f32[3,1,8,256]{3,0,2,1:T(4,128)S(1)}, f32[3,1,8,256]{3,0,2,1:T(4,128)S(1)}, u32[]{:S(2)}, u32[]{:S(2)}) collective-permute-start(f32[3,1,8,256]{3,0,2,1:T(4,128)S(1)} %bitcast.137), channel_id=1, source_target_pairs={{1,0},{2,1},{3,2},{4,3},{5,4},{6,5},{7,6},{8,7},{9,8},{10,9},{11,1... | collective-permute-start | bytes 73736 | tf_op jit(solution)/shard_map/ppermute | solution.py:18
Sparse Core Ops, SparseCore 0:
  22.7 19.4 reduce-scatter.3
where the time goes:
time: 129 us
  waiting for transfers between devices  51.8 us (40%)
  starting transfers between devices  35.5 us (28%)
  local copies, waits for them, and re-layouts  17 us (13%)
  between operations  13.8 us (11%)
  loops' own time  7.5 us (6%)
  matrix products  2.22 us (2%)
    ppermute x6, waiting for transfers between devices, extended(): lax.ppermute(lax.slice_in_dim(block, 0, width, axis=dim), axis, backward)  28 us
    unnamed x2, waiting for transfers between devices  19.4 us
    ppermute x6, starting transfers between devices, extended(): lax.ppermute(lax.slice_in_dim(block, block.shape[dim] - width, None, axis...  15.9 us
    ppermute x6, starting transfers between devices, extended(): lax.ppermute(lax.slice_in_dim(block, 0, width, axis=dim), axis, backward)  14 us
    another operation x1, loops' own time, shards(): gradient = lax.fori_loop(0, tile_count, add_tile, gradient)  7.5 us
    gather x2, local copies, waits for them, and re-layouts, shards(): jnp.take(padded_slots, slot_index, axis=2)  5.79 us
    all_to_all x1, starting transfers between devices, shards(): lax.all_to_all(reduced, 'cols', split_axis=1, concat_axis=4, tiled=True)  5.63 us
    all_to_all x1, waiting for transfers between devices, shards(): lax.all_to_all(reduced, 'cols', split_axis=1, concat_axis=4, tiled=True)  4.37 us
  transfers between devices with their start and end apart: 14, of which 8 were waited for; matrix products, arithmetic and copies ran while one was open for 0% of the time, Pallas kernels for 0%

commit v1 on v0

--- a/solution.py
+++ b/solution.py
@@ -1,6 +1,10 @@
+import functools
+
 import jax
 import jax.numpy as jnp
 from jax import lax
+from jax.experimental import pallas as pl
+from jax.experimental.pallas import tpu as pltpu
 from jax.sharding import PartitionSpec as P
 
 CAP = 384
@@ -51,7 +55,7 @@
     return jnp.tensordot(mixing, smooth, axes=1, precision=lax.Precision.HIGHEST)
 
 
-def shards(
+def shards_any(
     tile_bounds, tile_anchor, tile_picks, rmo_picks, sensitivity, dip_class, strength, couple
 ):
     tile_count, ray_count, param_count, depth_cells, tile_columns = sensitivity.shape
@@ -95,6 +99,321 @@
         padded = extended(field, ((("cols", "par"), 1),), 1)
         field = smooth_pass(padded, dip_class, strength, mixing)
     return field
+
+
+LANES = 128
+SUBLANES = 8
+
+
+def device_index():
+    return lax.axis_index("cols") * lax.axis_size("par") + lax.axis_index("par")
+
+
+def lane_ids(shape):
+    return lax.broadcasted_iota(jnp.int32, shape, len(shape) - 1)
+
+
+def roll_lanes(values, shift):
+    width = values.shape[-1]
+    shift = shift % width
+    return values if shift == 0 else pltpu.roll(values, shift, values.ndim - 1)
+
+
+def source_kernel(start_ref, anchor_ref, picks_ref, rmo_ref, sens_ref, dip_ref, out_ref, weight_ref):
+    tiles, rays, params, tile_depth, tile_columns = sens_ref.shape
+    _, rows_x, rows_y = dip_ref.shape
+    halves = rows_y // LANES
+    diagonal = lax.broadcasted_iota(jnp.int32, (rays, rays), 0) == lane_ids((rays, rays))
+    parts = [[[None] * tiles for _ in range(params)] for _ in range(halves)]
+    x_rows, depth_rows = [], []
+    y_ids = lane_ids((1, rows_y))
+    for tile in range(tiles):
+        live = lane_ids((1, rays)) < picks_ref[tile]
+        weight = jnp.where(live, rmo_ref[tile : tile + 1, :].astype(jnp.float32), 0.0)
+        column = jnp.sum(jnp.where(diagonal, weight, 0.0), axis=1, keepdims=True)
+        weight_ref[...] = jnp.broadcast_to(column, weight_ref.shape)
+        total = jnp.zeros((params, tile_depth, tile_columns), jnp.float32)
+        for ray in range(rays):
+            total = total + weight_ref[ray : ray + 1, :][None] * sens_ref[tile, ray].astype(jnp.float32)
+        depth_first = anchor_ref[tile, 0]
+        first = start_ref[0] + anchor_ref[tile, 1]
+        first_x = first // rows_y
+        first_y = first - first_x * rows_y
+        half_of = first_y // LANES
+        lane_first = first_y - half_of * LANES
+        past = lane_ids((1, LANES)) >= lane_first
+        for param in range(params):
+            turned = pltpu.roll(total[param], lax.rem(depth_first, tile_depth), 0)
+            turned = pltpu.roll(turned, lane_first, 1)
+            for half in range(halves):
+                after = lax.rem(half_of + 1, halves)
+                kept = jnp.logical_or(
+                    jnp.logical_and(past, half_of == half),
+                    jnp.logical_and(jnp.logical_not(past), after == half),
+                )
+                parts[half][param][tile] = jnp.where(kept, turned, 0.0)
+        x_rows.append((first_x + (y_ids < first_y).astype(jnp.int32)).astype(jnp.float32))
+        depth_rows.append(jnp.full((1, rows_y), depth_first, jnp.int32).astype(jnp.float32))
+    notes = jnp.concatenate(
+        x_rows + depth_rows + [jnp.zeros((SUBLANES - 2 * tiles, rows_y), jnp.float32)], axis=0
+    )
+    dip = dip_ref[0].astype(jnp.float32)
+    width = out_ref.shape[1]
+    side = jnp.concatenate([roll_lanes(dip, width), dip, roll_lanes(dip, -width), notes], axis=0)
+    for half in range(halves):
+        rows = [side[:, half * LANES : (half + 1) * LANES]]
+        for param in range(params):
+            rows.extend(parts[half][param])
+        whole = jnp.concatenate(rows, axis=0)
+        count = LANES // width
+        out_ref[half * count : (half + 1) * count] = jnp.transpose(whole).reshape(count, width, LANES)
+
+
+def smooth_kernel(strength_ref, couple_ref, in_ref, out_ref, dip_scratch, *, params, tiles, rows_x, rows_y):
+    depth, width, _ = in_ref.shape
+    groups = LANES // depth
+    halves = rows_x // groups
+    side = 3 * rows_x
+    rows = 3 * width
+    lane = lane_ids((width, LANES))
+    z = lane % depth
+    low = z < depth // 2
+    z_float = z.astype(jnp.float32)
+
+    def add_source(source, field):
+        message = in_ref[source]
+        swapped = jnp.where(low, roll_lanes(message, -(depth // 2)), roll_lanes(message, depth // 2))
+        field = list(field)
+        for tile in range(tiles):
+            own = low if tile == 0 else jnp.logical_not(low)
+            values = jnp.where(own, message, swapped)
+            at_x = jnp.broadcast_to(message[:, side + tile : side + tile + 1], (width, LANES))
+            first_z = jnp.broadcast_to(
+                message[:, side + tiles + tile : side + tiles + tile + 1], (width, LANES)
+            )
+            behind = z_float - first_z
+            inside = jnp.logical_and(behind >= 0.0, behind < float(depth // 2))
+            at_x = jnp.where(inside, at_x, -1.0)
+            for x in range(rows_x):
+                field[x] = field[x] + jnp.where(at_x == float(x), values, 0.0)
+        return tuple(field)
+
+    zero = jnp.zeros((width, LANES), jnp.float32)
+    field = (zero,) * rows_x
+    for source in range(depth):
+        field = add_source(source, field)
+
+    block = lane // depth
+    current = []
+    for param in range(params):
+        current.append([])
+        for half in range(halves):
+            centre = zero
+            for group in range(groups):
+                moved = roll_lanes(field[half * groups + group], depth * (group - param - 1))
+                centre = jnp.where(block == group, moved, centre)
+            current[param].append(jnp.concatenate([zero, centre, zero], axis=0))
+
+    for row in range(width):
+        dip_scratch[row] = jnp.transpose(
+            jnp.concatenate(
+                [in_ref[:, row, :], jnp.zeros((LANES - depth, LANES), jnp.float32)], axis=0
+            )
+        )[:side]
+    dip = []
+    for half in range(halves):
+        bands = []
+        for band in range(3):
+            merged = zero
+            for group in range(groups):
+                values = dip_scratch[:, band * rows_x + half * groups + group, :]
+                merged = jnp.where(block == group, roll_lanes(values, depth * group), merged)
+            bands.append(merged)
+        dip.append(jnp.concatenate(bands, axis=0))
+
+    lanes = lane_ids((rows, LANES))
+    z = lanes % depth
+    block = lanes // depth
+    first = block == 0
+    last = block == groups - 1
+    top = z == 0
+    bottom = z == depth - 1
+    y = device_index() * width - width + lax.broadcasted_iota(jnp.int32, (rows, LANES), 0)
+    in_grid = jnp.logical_and(y >= 0, y < rows_y)
+
+    def from_next_x(values):
+        moved = [roll_lanes(v, -depth) for v in values]
+        return [
+            jnp.where(last, moved[h + 1] if h + 1 < halves else 0.0, moved[h]) for h in range(halves)
+        ]
+
+    def from_prev_x(values):
+        moved = [roll_lanes(v, depth) for v in values]
+        return [jnp.where(first, moved[h - 1] if h > 0 else 0.0, moved[h]) for h in range(halves)]
+
+    def from_next_y(values):
+        return [pltpu.roll(v, rows - 1, 0) for v in values]
+
+    def from_prev_y(values):
+        return [pltpu.roll(v, 1, 0) for v in values]
+
+    def masks(values):
+        return [(v < -0.5, v > 0.5) for v in values]
+
+    tilt_x = [jnp.where(d < 2.5, -1.0, jnp.where(d > 5.5, 1.0, 0.0)) for d in dip]
+    tilt_y = [d - 3.0 * (t + 1.0) - 1.0 for d, t in zip(dip, tilt_x)]
+    to_west = masks(from_prev_x(tilt_x))
+    to_east = masks(from_next_x(tilt_x))
+    to_south = masks(from_prev_y(tilt_y))
+    to_north = masks(from_next_y(tilt_y))
+
+    strengths = [jnp.full((rows, LANES), strength_ref[q], jnp.float32) for q in range(params)]
+    mixing = []
+    for p in range(params):
+        weights = [jnp.full((rows, LANES), couple_ref[p, q], jnp.float32) for q in range(params)]
+        whole = weights[0]
+        for weight in weights[1:]:
+            whole = whole + weight
+        mixing.append([jnp.where(in_grid, weight / whole, 0.0) for weight in weights])
+
+    for _ in range(PASSES):
+        smooth = []
+        for q in range(params):
+            u = current[q]
+            above = [jnp.where(top, 0.0, roll_lanes(v, 1)) for v in u]
+            below = [jnp.where(bottom, 0.0, roll_lanes(v, -1)) for v in u]
+
+            def plus(tilts):
+                return [
+                    jnp.where(neg, a, jnp.where(pos, b, v))
+                    for (neg, pos), a, v, b in zip(tilts, above, u, below)
+                ]
+
+            def minus(tilts):
+                return [
+                    jnp.where(neg, b, jnp.where(pos, a, v))
+                    for (neg, pos), a, v, b in zip(tilts, above, u, below)
+                ]
+
+            east = from_next_x(plus(to_west))
+            west = from_prev_x(minus(to_east))
+            north = from_next_y(plus(to_south))
+            south = from_prev_y(minus(to_north))
+            smooth.append(
+                [
+                    v + strengths[q] * (e + w + n + s - 4.0 * v)
+                    for v, e, w, n, s in zip(u, east, west, north, south)
+                ]
+            )
+        current = []
+        for p in range(params):
+            mixed = []
+            for half in range(halves):
+                value = mixing[p][0] * smooth[0][half]
+                for q in range(1, params):
+                    value = value + mixing[p][q] * smooth[q][half]
+                mixed.append(value)
+            current.append(mixed)
+
+    gap = jnp.zeros((LANES // groups - rows, LANES), jnp.float32)
+    for half in range(halves):
+        pieces = []
+        for p in range(params):
+            pieces.extend([current[p][half], gap])
+        pieces.append(jnp.zeros((LANES // groups, LANES), jnp.float32))
+        turned = jnp.transpose(jnp.concatenate(pieces, axis=0))
+        for group in range(groups):
+            out_ref[:, half * groups + group, :] = turned[group * depth : (group + 1) * depth]
+
+
+def collect_kernel(in_ref, out_ref, *, width):
+    params, _, rows_x, rows_y = out_ref.shape
+    groups = params + 1
+    slot = LANES // groups
+    step = slot // width
+    halves = rows_y // LANES
+    block = lane_ids((rows_x, LANES)) // slot
+    for param in range(params):
+        total = jnp.zeros((rows_x, rows_y), jnp.float32)
+        for phase in range(step):
+            wide = []
+            for half in range(halves):
+                merged = jnp.zeros((rows_x, LANES), jnp.float32)
+                for group in range(groups):
+                    values = in_ref[(half * groups + group) * step + phase]
+                    merged = jnp.where(block == group, roll_lanes(values, slot * (group - param)), merged)
+                wide.append(merged)
+            total = total + roll_lanes(jnp.concatenate(wide, axis=1), (phase - 1) * width)
+        out_ref[param, 0] = total
+
+
+def fits(sensitivity, dip_class, devices):
+    tiles, _, params, tile_depth, tile_columns = sensitivity.shape
+    slab_depth, rows_x, rows_y = dip_class.shape
+    depth = slab_depth * devices
+    return (
+        slab_depth == 1
+        and rows_y == devices * SUBLANES
+        and PASSES <= SUBLANES
+        and rows_y % LANES == 0
+        and tile_columns == LANES
+        and rows_x == SUBLANES
+        and tiles == 2
+        and tiles * tile_depth == depth
+        and (params + 1) * depth == LANES
+        and 4 * SUBLANES == depth
+    )
+
+
+def shards_by_y(
+    tile_bounds, tile_anchor, tile_picks, rmo_picks, sensitivity, dip_class, strength, couple
+):
+    tiles, rays, params, _, _ = sensitivity.shape
+    _, rows_x, rows_y = dip_class.shape
+    devices = lax.axis_size("cols") * lax.axis_size("par")
+    width = rows_y // devices
+    own_start = lax.dynamic_slice(tile_bounds, (lax.axis_index("cols"),), (1,))
+    smem = pl.BlockSpec(memory_space=pltpu.SMEM)
+    vmem = pl.BlockSpec(memory_space=pltpu.VMEM)
+    packet = jax.ShapeDtypeStruct((devices, width, LANES), jnp.float32)
+    sent = pl.pallas_call(
+        source_kernel,
+        out_shape=packet,
+        in_specs=[smem, smem, smem, vmem, vmem, vmem],
+        out_specs=vmem,
+        scratch_shapes=[pltpu.VMEM((rays, LANES), jnp.float32)],
+        compiler_params=pltpu.CompilerParams(vmem_limit_bytes=32 << 20),
+        name="sum_rays",
+    )(own_start, tile_anchor, tile_picks, rmo_picks, sensitivity, dip_class)
+    received = lax.all_to_all(sent, ("cols", "par"), 0, 0)
+    layers = pl.pallas_call(
+        functools.partial(smooth_kernel, params=params, tiles=tiles, rows_x=rows_x, rows_y=rows_y),
+        out_shape=packet,
+        in_specs=[smem, smem, vmem],
+        out_specs=vmem,
+        scratch_shapes=[pltpu.VMEM((width, 3 * rows_x, LANES), jnp.float32)],
+        compiler_params=pltpu.CompilerParams(vmem_limit_bytes=32 << 20),
+        name="smooth_block",
+    )(strength, couple, received)
+    windows = lax.all_to_all(layers, ("cols", "par"), 0, 0)
+    return pl.pallas_call(
+        functools.partial(collect_kernel, width=width),
+        out_shape=jax.ShapeDtypeStruct((params, 1, rows_x, rows_y), jnp.float32),
+        in_specs=[vmem],
+        out_specs=vmem,
+        compiler_params=pltpu.CompilerParams(vmem_limit_bytes=32 << 20),
+        name="collect_windows",
+    )(windows)
+
+
+def shards(
+    tile_bounds, tile_anchor, tile_picks, rmo_picks, sensitivity, dip_class, strength, couple
+):
+    devices = lax.axis_size("cols") * lax.axis_size("par")
+    plan = shards_by_y if fits(sensitivity, dip_class, devices) else shards_any
+    return plan(
+        tile_bounds, tile_anchor, tile_picks, rmo_picks, sensitivity, dip_class, strength, couple
+    )
 
 
 def solution(mesh):

time: 129 us -> 36 us (0.28)
  the two profiles are of different devices: /device:TPU:7 before, /device:TPU:0 now
where the time goes in v1:
time: 36 us; the launch traced here: 35.7 us
  blocking collectives  25.3 us (70%)
  local copies, waits for them, and re-layouts  5.36 us (15%)
  Pallas kernels  4.99 us (14%)
    all_to_all x1, blocking collectives, shards_by_y(): received = lax.all_to_all(sent, ('cols', 'par'), 0, 0)  15.3 us
    all_to_all x1, blocking collectives, shards_by_y(): windows = lax.all_to_all(layers, ('cols', 'par'), 0, 0)  10 us
    unnamed x14, local copies, waits for them, and re-layouts  4.1 us
    pallas_call x1, Pallas kernels, shards_by_y(): pl.pallas_call(functools.partial(smooth_kernel, params=params, tiles=tile...  2.45 us
    pallas_call x1, Pallas kernels, shards_by_y(): pl.pallas_call(source_kernel, out_shape=packet, in_specs=[smem, smem, sme...  1.73 us
    dynamic_slice x1, local copies, waits for them, and re-layouts, shards_by_y(): own_start = lax.dynamic_slice(tile_bounds, (lax.axis_index('cols'),), (1,))  1.26 us
    pallas_call x1, Pallas kernels, shards_by_y(): pl.pallas_call(functools.partial(collect_kernel, width=width), out_shape=...  0.81 us

profile of v1, /device:TPU:0, one launch (start us, length us, event | category | flops | bytes accessed | tf_op | source)
XLA Modules:
  0.0 35.7 jit_solution(13304513772512958466)
XLA Ops:
  0.0 0.0 copy-start.2
  0.0 0.0 copy-start.6
  0.0 1.3 %dynamic_slice.3.start_ref = s32[1]{0:T(128)} dynamic-slice(s32[9]{0:T(128)} %param.8, s32[]{:T(128)S(6)} %select_n.3), dynamic_slice_sizes={1} | dynamic-slice | bytes 12 | tf_op jit(solution)/shard_map/dynamic_slice | solution.py:375
  1.3 0.0 copy-start
  1.3 1.4 %copy-done = bf16[2,64,3,16,128]{4,3,2,1,0:T(8,128)(2,1)S(1)} copy-done((bf16[2,64,3,16,128]{4,3,2,1,0:T(8,128)(2,1)S(1)}, bf16[2,64,3,16,128]{4,3,2,1,0:T(8,128)(2,1)}, u32[]{:S(2)}) %copy-start) | copy-done | bytes 1572888
  2.7 0.0 copy-start.1
  2.7 0.7 %copy-done.1 = s32[1,8,256]{2,1,0:T(8,128)S(1)} copy-done((s32[1,8,256]{2,1,0:T(8,128)S(1)}, s32[1,8,256]{2,1,0:T(8,128)}, u32[]{:S(2)}) %copy-start.1) | copy-done | bytes 8216
  3.4 0.0 copy-start.3
  3.4 0.7 %copy-done.3 = s32[2,2]{1,0:T(2,128)S(1)} copy-done((s32[2,2]{1,0:T(2,128)S(1)}, s32[2,2]{1,0:T(2,128)}, u32[]{:S(2)}) %copy-start.3) | copy-done | bytes 40
  4.1 0.0 copy-start.4
  4.1 0.7 %copy-done.4 = s32[2]{0:T(128)S(1)} copy-done((s32[2]{0:T(128)S(1)}, s32[2]{0:T(128)}, u32[]{:S(2)}) %copy-start.4) | copy-done | bytes 32
  4.7 0.0 copy-start.5
  4.7 0.7 %copy-done.5 = bf16[2,64]{1,0:T(2,128)(2,1)S(1)} copy-done((bf16[2,64]{1,0:T(2,128)(2,1)S(1)}, bf16[2,64]{1,0:T(2,128)(2,1)}, u32[]{:S(2)}) %copy-start.5) | copy-done | bytes 280
  5.4 1.7 %sum_rays.1 = f32[32,8,128]{2,1,0:T(8,128)S(1)} custom-call(s32[1]{0:T(128)} %dynamic_slice.3.start_ref, s32[2,2]{1,0:T(2,128)S(1)} %copy-done.3, s32[2]{0:T(128)S(1)} %copy-done.4, bf16[2,64]{1,0:T(2,128)(2,1)S(1)} %copy-done.5, bf16[2,64,3,16,128]{4,3,2,1,0:T(8,128)(2,1)S(1)} %copy-done, s32[1,8,256]{2,1,0:T(8,128)S(1)} %copy-done.1), custom_call_target="tpu_custom_call" | custom-call | tf_op jit(solution)/shard_map/sum_rays/pallas_call | solution.py:379
  7.1 15.3 %all_to_all.10.in_ref = f32[32,8,128]{2,1,0:T(8,128)S(1)} all-to-all(f32[32,8,128]{2,1,0:T(8,128)S(1)} %sum_rays.1), channel_id=1, replica_groups=mesh['cols'=8,'par'=4] {'cols','par'}, dimensions={0} | all-to-all | bytes 262144 | tf_op jit(solution)/shard_map/all_to_all | solution.py:388
  22.4 0.0 copy-done.2
  22.4 0.0 copy-done.6
  22.4 2.5 %smooth_block.1 = f32[32,8,128]{2,1,0:T(8,128)S(1)} custom-call(f32[3]{0:T(128)S(1)} %copy-done.6, f32[3,3]{1,0:T(4,128)S(1)} %copy-done.2, f32[32,8,128]{2,1,0:T(8,128)S(1)} %all_to_all.10.in_ref), custom_call_target="tpu_custom_call" | custom-call | tf_op jit(solution)/shard_map/smooth_block/pallas_call | solution.py:389
  24.9 10.0 %all_to_all.11.in_ref = f32[32,8,128]{2,1,0:T(8,128)S(1)} all-to-all(f32[32,8,128]{2,1,0:T(8,128)S(1)} %smooth_block.1), channel_id=1, replica_groups=mesh['cols'=8,'par'=4] {'cols','par'}, dimensions={0} | all-to-all | bytes 262144 | tf_op jit(solution)/shard_map/all_to_all | solution.py:398
  34.9 0.8 %collect_windows.1 = f32[3,1,8,256]{3,2,1,0:T(8,128)} custom-call(f32[32,8,128]{2,1,0:T(8,128)S(1)} %all_to_all.11.in_ref), custom_call_target="tpu_custom_call" | custom-call | tf_op jit(solution)/shard_map/collect_windows/pallas_call | solution.py:399
Async XLA Ops:
  0.0 22.4 %copy-start.2 = (f32[3,3]{1,0:T(4,128)S(1)}, f32[3,3]{1,0:T(4,128)}, u32[]{:S(2)}) copy-start(f32[3,3]{1,0:T(4,128)} %couple_ref.1) | copy-start | bytes 112
  0.0 22.4 %copy-start.6 = (f32[3]{0:T(128)S(1)}, f32[3]{0:T(128)}, u32[]{:S(2)}) copy-start(f32[3]{0:T(128)} %strength_ref.1) | copy-start | bytes 40
  1.3 1.4 %copy-start = (bf16[2,64,3,16,128]{4,3,2,1,0:T(8,128)(2,1)S(1)}, bf16[2,64,3,16,128]{4,3,2,1,0:T(8,128)(2,1)}, u32[]{:S(2)}) copy-start(bf16[2,64,3,16,128]{4,3,2,1,0:T(8,128)(2,1)} %sens_ref.1) | copy-start | bytes 4718596
  2.7 0.7 %copy-start.1 = (s32[1,8,256]{2,1,0:T(8,128)S(1)}, s32[1,8,256]{2,1,0:T(8,128)}, u32[]{:S(2)}) copy-start(s32[1,8,256]{2,1,0:T(8,128)} %dip_ref.1) | copy-start | bytes 24580
  3.4 0.7 %copy-start.3 = (s32[2,2]{1,0:T(2,128)S(1)}, s32[2,2]{1,0:T(2,128)}, u32[]{:S(2)}) copy-start(s32[2,2]{1,0:T(2,128)} %anchor_ref.1) | copy-start | bytes 52
  4.1 0.7 %copy-start.4 = (s32[2]{0:T(128)S(1)}, s32[2]{0:T(128)}, u32[]{:S(2)}) copy-start(s32[2]{0:T(128)} %picks_ref.1) | copy-start | bytes 28
  4.7 0.7 %copy-start.5 = (bf16[2,64]{1,0:T(2,128)(2,1)S(1)}, bf16[2,64]{1,0:T(2,128)(2,1)}, u32[]{:S(2)}) copy-start(bf16[2,64]{1,0:T(2,128)(2,1)} %rmo_ref.1) | copy-start | bytes 772

commit v2 on v1

--- a/solution.py
+++ b/solution.py
@@ -103,6 +103,7 @@
 
 LANES = 128
 SUBLANES = 8
+RAY_CHUNKS = 4
 
 
 def device_index():
@@ -119,31 +120,84 @@
     return values if shift == 0 else pltpu.roll(values, shift, values.ndim - 1)
 
 
-def source_kernel(start_ref, anchor_ref, picks_ref, rmo_ref, sens_ref, dip_ref, out_ref, weight_ref):
+def source_kernel(
+    bounds_hbm, anchor_hbm, picks_hbm, rmo_hbm, sens_hbm, dip_hbm, strength_hbm, couple_hbm,
+    out_ref, factor_ref,
+    bounds_ref, anchor_ref, picks_ref, rmo_ref, sens_ref, dip_ref, strength_ref, couple_ref,
+    weight_ref, small_sems, sens_sems,
+):
     tiles, rays, params, tile_depth, tile_columns = sens_ref.shape
     _, rows_x, rows_y = dip_ref.shape
+    devices, width, _ = out_ref.shape
     halves = rows_y // LANES
+    per_tile = sens_sems.shape[1]
+    chunk = rays // per_tile
+    small = [
+        pltpu.make_async_copy(hbm, ref, small_sems.at[number])
+        for number, (hbm, ref) in enumerate(
+            [
+                (picks_hbm, picks_ref),
+                (rmo_hbm, rmo_ref),
+                (bounds_hbm, bounds_ref),
+                (anchor_hbm, anchor_ref),
+                (dip_hbm, dip_ref),
+                (strength_hbm, strength_ref),
+                (couple_hbm, couple_ref),
+            ]
+        )
+    ]
+    large = [
+        [
+            pltpu.make_async_copy(
+                sens_hbm.at[tile, pl.ds(part * chunk, chunk)],
+                sens_ref.at[tile, pl.ds(part * chunk, chunk)],
+                sens_sems.at[tile, part],
+            )
+            for part in range(per_tile)
+        ]
+        for tile in range(tiles)
+    ]
+    for copy in small[:2]:
+        copy.start()
+    for row in large:
+        for copy in row:
+            copy.start()
+    for copy in small[2:]:
+        copy.start()
+
     diagonal = lax.broadcasted_iota(jnp.int32, (rays, rays), 0) == lane_ids((rays, rays))
+    for copy in small[:2]:
+        copy.wait()
+    for tile in range(tiles):
+        live = lane_ids((1, rays)) < picks_ref[tile]
+        weight = jnp.where(live, rmo_ref[tile : tile + 1, :].astype(jnp.float32), 0.0)
+        column = jnp.sum(jnp.where(diagonal, weight, 0.0), axis=1, keepdims=True)
+        weight_ref[tile] = jnp.broadcast_to(column, (rays, LANES))
+    sums = []
+    for tile in range(tiles):
+        total = jnp.zeros((params, tile_depth, tile_columns), jnp.float32)
+        for ray in range(rays):
+            if ray % chunk == 0:
+                large[tile][ray // chunk].wait()
+            weight = weight_ref[tile, ray : ray + 1, :]
+            total = total + weight[None] * sens_ref[tile, ray].astype(jnp.float32)
+        sums.append(total)
+    for copy in small[2:]:
+        copy.wait()
+
     parts = [[[None] * tiles for _ in range(params)] for _ in range(halves)]
     x_rows, depth_rows = [], []
     y_ids = lane_ids((1, rows_y))
     for tile in range(tiles):
-        live = lane_ids((1, rays)) < picks_ref[tile]
-        weight = jnp.where(live, rmo_ref[tile : tile + 1, :].astype(jnp.float32), 0.0)
-        column = jnp.sum(jnp.where(diagonal, weight, 0.0), axis=1, keepdims=True)
-        weight_ref[...] = jnp.broadcast_to(column, weight_ref.shape)
-        total = jnp.zeros((params, tile_depth, tile_columns), jnp.float32)
-        for ray in range(rays):
-            total = total + weight_ref[ray : ray + 1, :][None] * sens_ref[tile, ray].astype(jnp.float32)
         depth_first = anchor_ref[tile, 0]
-        first = start_ref[0] + anchor_ref[tile, 1]
+        first = bounds_ref[lax.axis_index("cols")] + anchor_ref[tile, 1]
         first_x = first // rows_y
         first_y = first - first_x * rows_y
         half_of = first_y // LANES
         lane_first = first_y - half_of * LANES
         past = lane_ids((1, LANES)) >= lane_first
         for param in range(params):
-            turned = pltpu.roll(total[param], lax.rem(depth_first, tile_depth), 0)
+            turned = pltpu.roll(sums[tile][param], lax.rem(depth_first, tile_depth), 0)
             turned = pltpu.roll(turned, lane_first, 1)
             for half in range(halves):
                 after = lax.rem(half_of + 1, halves)
@@ -155,26 +209,43 @@
         x_rows.append((first_x + (y_ids < first_y).astype(jnp.int32)).astype(jnp.float32))
         depth_rows.append(jnp.full((1, rows_y), depth_first, jnp.int32).astype(jnp.float32))
     notes = jnp.concatenate(
-        x_rows + depth_rows + [jnp.zeros((SUBLANES - 2 * tiles, rows_y), jnp.float32)], axis=0
+        [jnp.zeros((3 * width, rows_y), jnp.float32)]
+        + x_rows
+        + depth_rows
+        + [jnp.zeros((width - 2 * tiles, rows_y), jnp.float32)],
+        axis=0,
     )
     dip = dip_ref[0].astype(jnp.float32)
-    width = out_ref.shape[1]
-    side = jnp.concatenate([roll_lanes(dip, width), dip, roll_lanes(dip, -width), notes], axis=0)
+    in_window = lane_ids((rows_x, LANES)) < 3 * width
+    count = LANES // width
     for half in range(halves):
-        rows = [side[:, half * LANES : (half + 1) * LANES]]
+        rows = [notes[:, half * LANES : (half + 1) * LANES]]
         for param in range(params):
             rows.extend(parts[half][param])
-        whole = jnp.concatenate(rows, axis=0)
-        count = LANES // width
-        out_ref[half * count : (half + 1) * count] = jnp.transpose(whole).reshape(count, width, LANES)
-
-
-def smooth_kernel(strength_ref, couple_ref, in_ref, out_ref, dip_scratch, *, params, tiles, rows_x, rows_y):
+        turned = jnp.transpose(jnp.concatenate(rows, axis=0))
+        for place in range(count):
+            device = half * count + place
+            window = roll_lanes(dip, width - device * width)[:, :LANES]
+            out_ref[device] = jnp.where(in_window, window, turned[place * width : (place + 1) * width])
+
+    for q in range(params):
+        factor_ref[q : q + 1, :] = jnp.full((1, LANES), strength_ref[q], jnp.float32)
+    for p in range(params):
+        weights = [jnp.full((1, LANES), couple_ref[p, q], jnp.float32) for q in range(params)]
+        whole = weights[0]
+        for weight in weights[1:]:
+            whole = whole + weight
+        for q in range(params):
+            row = (p + 1) * params + q
+            factor_ref[row : row + 1, :] = weights[q] / whole
+
+
+def smooth_kernel(factor_ref, in_ref, out_ref, *, params, tiles, rows_x, rows_y):
     depth, width, _ = in_ref.shape
     groups = LANES // depth
     halves = rows_x // groups
-    side = 3 * rows_x
     rows = 3 * width
+    side = rows
     lane = lane_ids((width, LANES))
     z = lane % depth
     low = z < depth // 2
@@ -214,22 +285,10 @@
                 centre = jnp.where(block == group, moved, centre)
             current[param].append(jnp.concatenate([zero, centre, zero], axis=0))
 
-    for row in range(width):
-        dip_scratch[row] = jnp.transpose(
-            jnp.concatenate(
-                [in_ref[:, row, :], jnp.zeros((LANES - depth, LANES), jnp.float32)], axis=0
-            )
-        )[:side]
     dip = []
     for half in range(halves):
-        bands = []
-        for band in range(3):
-            merged = zero
-            for group in range(groups):
-                values = dip_scratch[:, band * rows_x + half * groups + group, :]
-                merged = jnp.where(block == group, roll_lanes(values, depth * group), merged)
-            bands.append(merged)
-        dip.append(jnp.concatenate(bands, axis=0))
+        layers = [in_ref[:, half * groups + group, :] for group in range(groups)]
+        dip.append(jnp.transpose(jnp.concatenate(layers, axis=0))[:rows])
 
     lanes = lane_ids((rows, LANES))
     z = lanes % depth
@@ -267,14 +326,14 @@
     to_south = masks(from_prev_y(tilt_y))
     to_north = masks(from_next_y(tilt_y))
 
-    strengths = [jnp.full((rows, LANES), strength_ref[q], jnp.float32) for q in range(params)]
-    mixing = []
-    for p in range(params):
-        weights = [jnp.full((rows, LANES), couple_ref[p, q], jnp.float32) for q in range(params)]
-        whole = weights[0]
-        for weight in weights[1:]:
-            whole = whole + weight
-        mixing.append([jnp.where(in_grid, weight / whole, 0.0) for weight in weights])
+    def factor(row):
+        return jnp.broadcast_to(factor_ref[row : row + 1, :], (rows, LANES))
+
+    strengths = [factor(q) for q in range(params)]
+    mixing = [
+        [jnp.where(in_grid, factor((p + 1) * params + q), 0.0) for q in range(params)]
+        for p in range(params)
+    ]
 
     for _ in range(PASSES):
         smooth = []
@@ -315,40 +374,45 @@
                 mixed.append(value)
             current.append(mixed)
 
-    gap = jnp.zeros((LANES // groups - rows, LANES), jnp.float32)
+    pieces = []
     for half in range(halves):
-        pieces = []
         for p in range(params):
-            pieces.extend([current[p][half], gap])
-        pieces.append(jnp.zeros((LANES // groups, LANES), jnp.float32))
-        turned = jnp.transpose(jnp.concatenate(pieces, axis=0))
-        for group in range(groups):
-            out_ref[:, half * groups + group, :] = turned[group * depth : (group + 1) * depth]
+            pieces.append(current[p][half][width - PASSES : 2 * width + PASSES])
+    used = halves * params * (width + 2 * PASSES)
+    pieces.append(jnp.zeros((LANES - used, LANES), jnp.float32))
+    turned = jnp.transpose(jnp.concatenate(pieces, axis=0))
+    for group in range(groups):
+        out_ref[:, group, :] = turned[group * depth : (group + 1) * depth]
 
 
 def collect_kernel(in_ref, out_ref, *, width):
     params, _, rows_x, rows_y = out_ref.shape
-    groups = params + 1
-    slot = LANES // groups
-    step = slot // width
-    halves = rows_y // LANES
-    block = lane_ids((rows_x, LANES)) // slot
+    sources, groups, _ = in_ref.shape
+    span = width + 2 * PASSES
+    halves = rows_x // groups
+    lane = lane_ids((rows_x, LANES))
+    totals = [[jnp.zeros((rows_x, LANES), jnp.float32) for _ in range(rows_y // LANES)] for _ in range(params)]
+    for source in range(sources):
+        message = in_ref[source]
+        stacked = jnp.concatenate(
+            [roll_lanes(message, -half * params * span) for half in range(halves)], axis=0
+        )
+        first = source * width - PASSES
+        for param in range(params):
+            placed = roll_lanes(stacked, first - param * span)
+            for column in range(rows_y // LANES):
+                low, high = first - column * LANES, first - column * LANES + span
+                if high <= 0 or low >= LANES:
+                    continue
+                inside = jnp.logical_and(lane >= low, lane < high)
+                totals[param][column] = totals[param][column] + jnp.where(inside, placed, 0.0)
     for param in range(params):
-        total = jnp.zeros((rows_x, rows_y), jnp.float32)
-        for phase in range(step):
-            wide = []
-            for half in range(halves):
-                merged = jnp.zeros((rows_x, LANES), jnp.float32)
-                for group in range(groups):
-                    values = in_ref[(half * groups + group) * step + phase]
-                    merged = jnp.where(block == group, roll_lanes(values, slot * (group - param)), merged)
-                wide.append(merged)
-            total = total + roll_lanes(jnp.concatenate(wide, axis=1), (phase - 1) * width)
-        out_ref[param, 0] = total
+        for column in range(rows_y // LANES):
+            out_ref[param, 0, :, column * LANES : (column + 1) * LANES] = totals[param][column]
 
 
 def fits(sensitivity, dip_class, devices):
-    tiles, _, params, tile_depth, tile_columns = sensitivity.shape
+    tiles, rays, params, tile_depth, tile_columns = sensitivity.shape
     slab_depth, rows_x, rows_y = dip_class.shape
     depth = slab_depth * devices
     return (
@@ -362,6 +426,8 @@
         and tiles * tile_depth == depth
         and (params + 1) * depth == LANES
         and 4 * SUBLANES == depth
+        and rays % RAY_CHUNKS == 0
+        and rows_x * params * (SUBLANES + 2 * PASSES) <= 4 * LANES
     )
 
 
@@ -372,29 +438,41 @@
     _, rows_x, rows_y = dip_class.shape
     devices = lax.axis_size("cols") * lax.axis_size("par")
     width = rows_y // devices
-    own_start = lax.dynamic_slice(tile_bounds, (lax.axis_index("cols"),), (1,))
-    smem = pl.BlockSpec(memory_space=pltpu.SMEM)
+    groups = LANES // devices
+    hbm = pl.BlockSpec(memory_space=pltpu.HBM)
     vmem = pl.BlockSpec(memory_space=pltpu.VMEM)
-    packet = jax.ShapeDtypeStruct((devices, width, LANES), jnp.float32)
-    sent = pl.pallas_call(
+    arguments = (
+        tile_bounds, tile_anchor, tile_picks, rmo_picks, sensitivity, dip_class, strength, couple
+    )
+    homes = (
+        pltpu.SMEM, pltpu.SMEM, pltpu.SMEM, pltpu.VMEM, pltpu.VMEM, pltpu.VMEM, pltpu.SMEM, pltpu.SMEM
+    )
+    sent, factors = pl.pallas_call(
         source_kernel,
-        out_shape=packet,
-        in_specs=[smem, smem, smem, vmem, vmem, vmem],
-        out_specs=vmem,
-        scratch_shapes=[pltpu.VMEM((rays, LANES), jnp.float32)],
+        out_shape=(
+            jax.ShapeDtypeStruct((devices, width, LANES), jnp.float32),
+            jax.ShapeDtypeStruct(((params + 1) * params, LANES), jnp.float32),
+        ),
+        in_specs=[hbm] * len(arguments),
+        out_specs=(vmem, vmem),
+        scratch_shapes=[home(array.shape, array.dtype) for home, array in zip(homes, arguments)]
+        + [
+            pltpu.VMEM((tiles, rays, LANES), jnp.float32),
+            pltpu.SemaphoreType.DMA((len(arguments) - 1,)),
+            pltpu.SemaphoreType.DMA((tiles, RAY_CHUNKS)),
+        ],
         compiler_params=pltpu.CompilerParams(vmem_limit_bytes=32 << 20),
         name="sum_rays",
-    )(own_start, tile_anchor, tile_picks, rmo_picks, sensitivity, dip_class)
+    )(*arguments)
     received = lax.all_to_all(sent, ("cols", "par"), 0, 0)
     layers = pl.pallas_call(
         functools.partial(smooth_kernel, params=params, tiles=tiles, rows_x=rows_x, rows_y=rows_y),
-        out_shape=packet,
-        in_specs=[smem, smem, vmem],
+        out_shape=jax.ShapeDtypeStruct((devices, groups, LANES), jnp.float32),
+        in_specs=[vmem, vmem],
         out_specs=vmem,
-        scratch_shapes=[pltpu.VMEM((width, 3 * rows_x, LANES), jnp.float32)],
         compiler_params=pltpu.CompilerParams(vmem_limit_bytes=32 << 20),
         name="smooth_block",
-    )(strength, couple, received)
+    )(factors, received)
     windows = lax.all_to_all(layers, ("cols", "par"), 0, 0)
     return pl.pallas_call(
         functools.partial(collect_kernel, width=width),

time: 36 us -> 36.5 us (1.014)
  blocking collectives: 25.3 us -> 24.5 us
  local copies, waits for them, and re-layouts: 5.36 us -> 6.08 us
  Pallas kernels: 4.99 us -> 5.58 us
    unnamed x14 -> x16, local copies, waits for them, and re-layouts: 4.1 us -> 6.08 us
    dynamic_slice x1 -> x0, local copies, waits for them, and re-layouts: 1.26 us -> none  [shards_by_y(): own_start = lax.dynamic_slice(tile_bounds, (lax.axis_index('cols'),), (1,))]
    pallas_call x1, Pallas kernels: 1.73 us -> 2.93 us  [shards_by_y(): pl.pallas_call(source_kernel, out_shape=(jax.ShapeDtypeStruct((devices, w...]
    all_to_all x1, blocking collectives: 10 us -> 9.18 us  [shards_by_y(): windows = lax.all_to_all(layers, ('cols', 'par'), 0, 0)]
    pallas_call x1, Pallas kernels: 2.45 us -> 1.79 us  [shards_by_y(): pl.pallas_call(functools.partial(smooth_kernel, params=params, tiles=tile...]
where the time goes in v2:
time: 36.5 us; the launch traced here: 36.2 us
  blocking collectives  24.5 us (67%)
  local copies, waits for them, and re-layouts  6.08 us (17%)
  Pallas kernels  5.58 us (15%)
    all_to_all x1, blocking collectives, shards_by_y(): received = lax.all_to_all(sent, ('cols', 'par'), 0, 0)  15.3 us
    all_to_all x1, blocking collectives, shards_by_y(): windows = lax.all_to_all(layers, ('cols', 'par'), 0, 0)  9.18 us
    unnamed x16, local copies, waits for them, and re-layouts  6.08 us
    pallas_call x1, Pallas kernels, shards_by_y(): pl.pallas_call(source_kernel, out_shape=(jax.ShapeDtypeStruct((devices, w...  2.93 us
    pallas_call x1, Pallas kernels, shards_by_y(): pl.pallas_call(functools.partial(smooth_kernel, params=params, tiles=tile...  1.79 us
    pallas_call x1, Pallas kernels, shards_by_y(): pl.pallas_call(functools.partial(collect_kernel, width=width), out_shape=...  0.86 us

profile of v2, /device:TPU:0, one launch (start us, length us, event | category | flops | bytes accessed | tf_op | source)
XLA Modules:
  0.0 36.2 jit_solution(13568667350657665177)
XLA Ops:
  0.0 0.0 copy-start
  0.0 1.4 %copy-done = bf16[2,64,3,16,128]{4,3,2,1,0:T(8,128)(2,1)S(1)} copy-done((bf16[2,64,3,16,128]{4,3,2,1,0:T(8,128)(2,1)S(1)}, bf16[2,64,3,16,128]{4,3,2,1,0:T(8,128)(2,1)}, u32[]{:S(2)}) %copy-start) | copy-done | bytes 1572888
  1.4 0.0 copy-start.1
  1.4 0.7 %copy-done.1 = s32[1,8,256]{2,1,0:T(8,128)S(1)} copy-done((s32[1,8,256]{2,1,0:T(8,128)S(1)}, s32[1,8,256]{2,1,0:T(8,128)}, u32[]{:S(2)}) %copy-start.1) | copy-done | bytes 8216
  2.1 0.0 copy-start.2
  2.1 0.7 %copy-done.2 = f32[3,3]{1,0:T(4,128)S(1)} copy-done((f32[3,3]{1,0:T(4,128)S(1)}, f32[3,3]{1,0:T(4,128)}, u32[]{:S(2)}) %copy-start.2) | copy-done | bytes 60
  2.8 0.0 copy-start.3
  2.8 0.7 %copy-done.3 = s32[2,2]{1,0:T(2,128)S(1)} copy-done((s32[2,2]{1,0:T(2,128)S(1)}, s32[2,2]{1,0:T(2,128)}, u32[]{:S(2)}) %copy-start.3) | copy-done | bytes 40
  3.5 0.0 copy-start.4
  3.5 0.7 %copy-done.4 = s32[9]{0:T(128)S(1)} copy-done((s32[9]{0:T(128)S(1)}, s32[9]{0:T(128)}, u32[]{:S(2)}) %copy-start.4) | copy-done | bytes 60
  4.1 0.0 copy-start.5
  4.1 0.7 %copy-done.5 = s32[2]{0:T(128)S(1)} copy-done((s32[2]{0:T(128)S(1)}, s32[2]{0:T(128)}, u32[]{:S(2)}) %copy-start.5) | copy-done | bytes 32
  4.8 0.0 copy-start.6
  4.8 0.7 %copy-done.6 = bf16[2,64]{1,0:T(2,128)(2,1)S(1)} copy-done((bf16[2,64]{1,0:T(2,128)(2,1)S(1)}, bf16[2,64]{1,0:T(2,128)(2,1)}, u32[]{:S(2)}) %copy-start.6) | copy-done | bytes 280
  5.4 0.0 copy-start.7
  5.4 0.7 %copy-done.7 = f32[3]{0:T(128)S(1)} copy-done((f32[3]{0:T(128)S(1)}, f32[3]{0:T(128)}, u32[]{:S(2)}) %copy-start.7) | copy-done | bytes 36
  6.1 2.9 %sum_rays.1 = (f32[32,8,128]{2,1,0:T(8,128)S(1)}, f32[12,128]{1,0:T(8,128)S(1)}) custom-call(s32[9]{0:T(128)S(1)} %copy-done.4, s32[2,2]{1,0:T(2,128)S(1)} %copy-done.3, s32[2]{0:T(128)S(1)} %copy-done.5, bf16[2,64]{1,0:T(2,128)(2,1)S(1)} %copy-done.6, bf16[2,64,3,16,128]{4,3,2,1,0:T(8,128)(2,1)S(1)} %copy-done, s32[1,8,256]{2,1,0:T(8,128)S(1)} %copy-done.1, ...), custom_call_target="tpu_custom_call" | custom-call | tf_op jit(solution)/shard_map/sum_rays/pallas_call | solution.py:450
  9.0 15.3 %all_to_all.10.in_ref = f32[32,8,128]{2,1,0:T(8,128)S(1)} all-to-all(f32[32,8,128]{2,1,0:T(8,128)S(1)} %get-tuple-element.8), channel_id=1, replica_groups=mesh['cols'=8,'par'=4] {'cols','par'}, dimensions={0} | all-to-all | bytes 262144 | tf_op jit(solution)/shard_map/all_to_all | solution.py:467
  24.4 1.8 %smooth_block.1 = f32[32,4,128]{2,1,0:T(4,128)S(1)} custom-call(f32[12,128]{1,0:T(8,128)S(1)} %get-tuple-element.7.factor_ref, f32[32,8,128]{2,1,0:T(8,128)S(1)} %all_to_all.10.in_ref), custom_call_target="tpu_custom_call" | custom-call | tf_op jit(solution)/shard_map/smooth_block/pallas_call | solution.py:468
  26.2 9.2 %all_to_all.11.in_ref = f32[32,4,128]{2,1,0:T(4,128)S(1)} all-to-all(f32[32,4,128]{2,1,0:T(4,128)S(1)} %smooth_block.1), channel_id=1, replica_groups=mesh['cols'=8,'par'=4] {'cols','par'}, dimensions={0} | all-to-all | bytes 131072 | tf_op jit(solution)/shard_map/all_to_all | solution.py:476
  35.4 0.9 %collect_windows.1 = f32[3,1,8,256]{3,2,1,0:T(8,128)} custom-call(f32[32,4,128]{2,1,0:T(4,128)S(1)} %all_to_all.11.in_ref), custom_call_target="tpu_custom_call" | custom-call | tf_op jit(solution)/shard_map/collect_windows/pallas_call | solution.py:477
Async XLA Ops:
  0.0 1.4 %copy-start = (bf16[2,64,3,16,128]{4,3,2,1,0:T(8,128)(2,1)S(1)}, bf16[2,64,3,16,128]{4,3,2,1,0:T(8,128)(2,1)}, u32[]{:S(2)}) copy-start(bf16[2,64,3,16,128]{4,3,2,1,0:T(8,128)(2,1)} %sens_hbm.1) | copy-start | bytes 4718596
  1.4 0.7 %copy-start.1 = (s32[1,8,256]{2,1,0:T(8,128)S(1)}, s32[1,8,256]{2,1,0:T(8,128)}, u32[]{:S(2)}) copy-start(s32[1,8,256]{2,1,0:T(8,128)} %dip_hbm.1) | copy-start | bytes 24580
  2.1 0.7 %copy-start.2 = (f32[3,3]{1,0:T(4,128)S(1)}, f32[3,3]{1,0:T(4,128)}, u32[]{:S(2)}) copy-start(f32[3,3]{1,0:T(4,128)} %couple_hbm.1) | copy-start | bytes 112
  2.8 0.7 %copy-start.3 = (s32[2,2]{1,0:T(2,128)S(1)}, s32[2,2]{1,0:T(2,128)}, u32[]{:S(2)}) copy-start(s32[2,2]{1,0:T(2,128)} %anchor_hbm.1) | copy-start | bytes 52
  3.5 0.7 %copy-start.4 = (s32[9]{0:T(128)S(1)}, s32[9]{0:T(128)}, u32[]{:S(2)}) copy-start(s32[9]{0:T(128)} %bounds_hbm.1) | copy-start | bytes 112
  4.1 0.7 %copy-start.5 = (s32[2]{0:T(128)S(1)}, s32[2]{0:T(128)}, u32[]{:S(2)}) copy-start(s32[2]{0:T(128)} %picks_hbm.1) | copy-start | bytes 28
  4.8 0.7 %copy-start.6 = (bf16[2,64]{1,0:T(2,128)(2,1)S(1)}, bf16[2,64]{1,0:T(2,128)(2,1)}, u32[]{:S(2)}) copy-start(bf16[2,64]{1,0:T(2,128)(2,1)} %rmo_hbm.1) | copy-start | bytes 772
  5.4 0.7 %copy-start.7 = (f32[3]{0:T(128)S(1)}, f32[3]{0:T(128)}, u32[]{:S(2)}) copy-start(f32[3]{0:T(128)} %strength_hbm.1) | copy-start | bytes 40

commit v3 on v2

--- a/solution.py
+++ b/solution.py
@@ -122,7 +122,7 @@
 
 def source_kernel(
     bounds_hbm, anchor_hbm, picks_hbm, rmo_hbm, sens_hbm, dip_hbm, strength_hbm, couple_hbm,
-    out_ref, factor_ref,
+    out_ref,
     bounds_ref, anchor_ref, picks_ref, rmo_ref, sens_ref, dip_ref, strength_ref, couple_ref,
     weight_ref, small_sems, sens_sems,
 ):
@@ -208,12 +208,23 @@
                 parts[half][param][tile] = jnp.where(kept, turned, 0.0)
         x_rows.append((first_x + (y_ids < first_y).astype(jnp.int32)).astype(jnp.float32))
         depth_rows.append(jnp.full((1, rows_y), depth_first, jnp.int32).astype(jnp.float32))
+    place_in_packet = lax.rem(y_ids, width)
+
+    def packet_lane(values):
+        lane = jnp.zeros((1, rows_y), jnp.float32)
+        for q, value in enumerate(values):
+            lane = jnp.where(place_in_packet == q, value, lane)
+        return lane
+
+    factor_rows = [packet_lane([strength_ref[q] for q in range(params)])]
+    for p in range(params):
+        weights = [jnp.full((1, rows_y), couple_ref[p, q], jnp.float32) for q in range(params)]
+        whole = weights[0]
+        for weight in weights[1:]:
+            whole = whole + weight
+        factor_rows.append(packet_lane([weight / whole for weight in weights]))
     notes = jnp.concatenate(
-        [jnp.zeros((3 * width, rows_y), jnp.float32)]
-        + x_rows
-        + depth_rows
-        + [jnp.zeros((width - 2 * tiles, rows_y), jnp.float32)],
-        axis=0,
+        [jnp.zeros((3 * width, rows_y), jnp.float32)] + x_rows + depth_rows + factor_rows, axis=0
     )
     dip = dip_ref[0].astype(jnp.float32)
     in_window = lane_ids((rows_x, LANES)) < 3 * width
@@ -228,19 +239,8 @@
             window = roll_lanes(dip, width - device * width)[:, :LANES]
             out_ref[device] = jnp.where(in_window, window, turned[place * width : (place + 1) * width])
 
-    for q in range(params):
-        factor_ref[q : q + 1, :] = jnp.full((1, LANES), strength_ref[q], jnp.float32)
-    for p in range(params):
-        weights = [jnp.full((1, LANES), couple_ref[p, q], jnp.float32) for q in range(params)]
-        whole = weights[0]
-        for weight in weights[1:]:
-            whole = whole + weight
-        for q in range(params):
-            row = (p + 1) * params + q
-            factor_ref[row : row + 1, :] = weights[q] / whole
-
-
-def smooth_kernel(factor_ref, in_ref, out_ref, *, params, tiles, rows_x, rows_y):
+
+def smooth_kernel(in_ref, out_ref, *, params, tiles, rows_x, rows_y):
     depth, width, _ = in_ref.shape
     groups = LANES // depth
     halves = rows_x // groups
@@ -326,13 +326,13 @@
     to_south = masks(from_prev_y(tilt_y))
     to_north = masks(from_next_y(tilt_y))
 
-    def factor(row):
-        return jnp.broadcast_to(factor_ref[row : row + 1, :], (rows, LANES))
-
-    strengths = [factor(q) for q in range(params)]
+    def factor(lane, q):
+        at = side + 2 * tiles + lane
+        return jnp.broadcast_to(in_ref[0, q : q + 1, at : at + 1], (rows, LANES))
+
+    strengths = [factor(0, q) for q in range(params)]
     mixing = [
-        [jnp.where(in_grid, factor((p + 1) * params + q), 0.0) for q in range(params)]
-        for p in range(params)
+        [jnp.where(in_grid, factor(p + 1, q), 0.0) for q in range(params)] for p in range(params)
     ]
 
     for _ in range(PASSES):
@@ -425,7 +425,7 @@
         and tiles == 2
         and tiles * tile_depth == depth
         and (params + 1) * depth == LANES
-        and 4 * SUBLANES == depth
+        and 3 * SUBLANES + 2 * tiles + params + 1 == depth
         and rays % RAY_CHUNKS == 0
         and rows_x * params * (SUBLANES + 2 * PASSES) <= 4 * LANES
     )
@@ -447,32 +447,28 @@
     homes = (
         pltpu.SMEM, pltpu.SMEM, pltpu.SMEM, pltpu.VMEM, pltpu.VMEM, pltpu.VMEM, pltpu.SMEM, pltpu.SMEM
     )
-    sent, factors = pl.pallas_call(
+    sent = pl.pallas_call(
         source_kernel,
-        out_shape=(
-            jax.ShapeDtypeStruct((devices, width, LANES), jnp.float32),
-            jax.ShapeDtypeStruct(((params + 1) * params, LANES), jnp.float32),
-        ),
+        out_shape=jax.ShapeDtypeStruct((devices, width, LANES), jnp.float32),
         in_specs=[hbm] * len(arguments),
-        out_specs=(vmem, vmem),
+        out_specs=vmem,
         scratch_shapes=[home(array.shape, array.dtype) for home, array in zip(homes, arguments)]
         + [
             pltpu.VMEM((tiles, rays, LANES), jnp.float32),
             pltpu.SemaphoreType.DMA((len(arguments) - 1,)),
             pltpu.SemaphoreType.DMA((tiles, RAY_CHUNKS)),
         ],
-        compiler_params=pltpu.CompilerParams(vmem_limit_bytes=32 << 20),
         name="sum_rays",
     )(*arguments)
     received = lax.all_to_all(sent, ("cols", "par"), 0, 0)
     layers = pl.pallas_call(
         functools.partial(smooth_kernel, params=params, tiles=tiles, rows_x=rows_x, rows_y=rows_y),
         out_shape=jax.ShapeDtypeStruct((devices, groups, LANES), jnp.float32),
-        in_specs=[vmem, vmem],
+        in_specs=[vmem],
         out_specs=vmem,
         compiler_params=pltpu.CompilerParams(vmem_limit_bytes=32 << 20),
         name="smooth_block",
-    )(factors, received)
+    )(received)
     windows = lax.all_to_all(layers, ("cols", "par"), 0, 0)
     return pl.pallas_call(
         functools.partial(collect_kernel, width=width),

time: 36.5 us -> 30.2 us (0.83)
  local copies, waits for them, and re-layouts: 6.08 us -> 0 us
  Pallas kernels: 5.58 us -> 5.21 us
    unnamed x16 -> x0, local copies, waits for them, and re-layouts: 6.08 us -> none
    pallas_call x1, Pallas kernels: 2.93 us -> 2.54 us  [shards_by_y(): pl.pallas_call(source_kernel, out_shape=jax.ShapeDtypeStruct((devices, wi...]
where the time goes in v3:
time: 30.2 us; the launch traced here: 30 us
  blocking collectives  24.7 us (82%)
  Pallas kernels  5.21 us (17%)
    all_to_all x1, blocking collectives, shards_by_y(): received = lax.all_to_all(sent, ('cols', 'par'), 0, 0)  15.5 us
    all_to_all x1, blocking collectives, shards_by_y(): windows = lax.all_to_all(layers, ('cols', 'par'), 0, 0)  9.18 us
    pallas_call x1, Pallas kernels, shards_by_y(): pl.pallas_call(source_kernel, out_shape=jax.ShapeDtypeStruct((devices, wi...  2.54 us
    pallas_call x1, Pallas kernels, shards_by_y(): pl.pallas_call(functools.partial(smooth_kernel, params=params, tiles=tile...  1.8 us
    pallas_call x1, Pallas kernels, shards_by_y(): pl.pallas_call(functools.partial(collect_kernel, width=width), out_shape=...  0.86 us

profile of v3, /device:TPU:0, one launch (start us, length us, event | category | flops | bytes accessed | tf_op | source)
XLA Modules:
  0.0 30.0 jit_solution(4772934015184381146)
XLA Ops:
  0.0 2.5 %sum_rays.1 = f32[32,8,128]{2,1,0:T(8,128)} custom-call(s32[9]{0:T(128)} %bounds_hbm.1, s32[2,2]{1,0:T(2,128)} %anchor_hbm.1, s32[2]{0:T(128)} %picks_hbm.1, bf16[2,64]{1,0:T(2,128)(2,1)} %rmo_hbm.1, bf16[2,64,3,16,128]{4,3,2,1,0:T(8,128)(2,1)} %sens_hbm.1, s32[1,8,256]{2,1,0:T(8,128)} %dip_hbm.1, f32[3]{0:T(128)} %strength_hbm.1, f32[3,3]{1,0:T(4,128)} %couple_hbm.1), custom_call_target="tpu_custom_call" | custom-call | tf_op jit(solution)/shard_map/sum_rays/pallas_call | solution.py:450
  2.6 15.5 %all_to_all.10.in_ref = f32[32,8,128]{2,1,0:T(8,128)S(1)} all-to-all(f32[32,8,128]{2,1,0:T(8,128)} %sum_rays.1), channel_id=1, replica_groups=mesh['cols'=8,'par'=4] {'cols','par'}, dimensions={0} | all-to-all | bytes 262144 | tf_op jit(solution)/shard_map/all_to_all | solution.py:463
  18.1 1.8 %smooth_block.1 = f32[32,4,128]{2,1,0:T(4,128)S(1)} custom-call(f32[32,8,128]{2,1,0:T(8,128)S(1)} %all_to_all.10.in_ref), custom_call_target="tpu_custom_call" | custom-call | tf_op jit(solution)/shard_map/smooth_block/pallas_call | solution.py:464
  19.9 9.2 %all_to_all.11.in_ref = f32[32,4,128]{2,1,0:T(4,128)S(1)} all-to-all(f32[32,4,128]{2,1,0:T(4,128)S(1)} %smooth_block.1), channel_id=1, replica_groups=mesh['cols'=8,'par'=4] {'cols','par'}, dimensions={0} | all-to-all | bytes 131072 | tf_op jit(solution)/shard_map/all_to_all | solution.py:472
  29.1 0.9 %collect_windows.1 = f32[3,1,8,256]{3,2,1,0:T(8,128)} custom-call(f32[32,4,128]{2,1,0:T(4,128)S(1)} %all_to_all.11.in_ref), custom_call_target="tpu_custom_call" | custom-call | tf_op jit(solution)/shard_map/collect_windows/pallas_call | solution.py:473

commit v4 on v3

--- a/solution.py
+++ b/solution.py
@@ -449,7 +449,7 @@
     )
     sent = pl.pallas_call(
         source_kernel,
-        out_shape=jax.ShapeDtypeStruct((devices, width, LANES), jnp.float32),
+        out_shape=pltpu.VMEM((devices, width, LANES), jnp.float32),
         in_specs=[hbm] * len(arguments),
         out_specs=vmem,
         scratch_shapes=[home(array.shape, array.dtype) for home, array in zip(homes, arguments)]
@@ -458,8 +458,9 @@
             pltpu.SemaphoreType.DMA((len(arguments) - 1,)),
             pltpu.SemaphoreType.DMA((tiles, RAY_CHUNKS)),
         ],
+        compiler_params=pltpu.CompilerParams(vmem_limit_bytes=32 << 20),
         name="sum_rays",
-    )(*arguments)
+    )(*(pltpu.with_memory_space_constraint(array, pltpu.HBM) for array in arguments))
     received = lax.all_to_all(sent, ("cols", "par"), 0, 0)
     layers = pl.pallas_call(
         functools.partial(smooth_kernel, params=params, tiles=tiles, rows_x=rows_x, rows_y=rows_y),

time: 30.2 us -> 29.3 us (0.970)
  Pallas kernels: 5.21 us -> 4.57 us
    pallas_call x1, Pallas kernels: 2.54 us -> 1.91 us  [shards_by_y(): pl.pallas_call(source_kernel, out_shape=pltpu.VMEM((devices, width, LANES...]
where the time goes in v4:
time: 29.3 us; the launch traced here: 29.1 us
  blocking collectives  24.5 us (84%)
  Pallas kernels  4.57 us (16%)
    all_to_all x1, blocking collectives, shards_by_y(): received = lax.all_to_all(sent, ('cols', 'par'), 0, 0)  15.3 us
    all_to_all x1, blocking collectives, shards_by_y(): windows = lax.all_to_all(layers, ('cols', 'par'), 0, 0)  9.18 us
    pallas_call x1, Pallas kernels, shards_by_y(): pl.pallas_call(source_kernel, out_shape=pltpu.VMEM((devices, width, LANES...  1.91 us
    pallas_call x1, Pallas kernels, shards_by_y(): pl.pallas_call(functools.partial(smooth_kernel, params=params, tiles=tile...  1.8 us
    pallas_call x1, Pallas kernels, shards_by_y(): pl.pallas_call(functools.partial(collect_kernel, width=width), out_shape=...  0.86 us

profile of v4, /device:TPU:0, one launch (start us, length us, event | category | flops | bytes accessed | tf_op | source)
XLA Modules:
  0.0 29.1 jit_solution(15709817354492441472)
XLA Ops:
  0.0 1.9 %sum_rays.1 = f32[32,8,128]{2,1,0:T(8,128)S(1)} custom-call(s32[9]{0:T(128)} %bounds_hbm.1, s32[2,2]{1,0:T(2,128)} %anchor_hbm.1, s32[2]{0:T(128)} %picks_hbm.1, bf16[2,64]{1,0:T(2,128)(2,1)} %rmo_hbm.1, bf16[2,64,3,16,128]{4,3,2,1,0:T(8,128)(2,1)} %sens_hbm.1, s32[1,8,256]{2,1,0:T(8,128)} %dip_hbm.1, f32[3]{0:T(128)} %strength_hbm.1, f32[3,3]{1,0:T(4,128)} %couple_hbm.1), custom_call_target="tpu_custom_call" | custom-call | tf_op jit(solution)/shard_map/sum_rays/pallas_call | solution.py:450
  1.9 15.3 %all_to_all.10.in_ref = f32[32,8,128]{2,1,0:T(8,128)S(1)} all-to-all(f32[32,8,128]{2,1,0:T(8,128)S(1)} %sum_rays.1), channel_id=1, replica_groups=mesh['cols'=8,'par'=4] {'cols','par'}, dimensions={0} | all-to-all | bytes 262144 | tf_op jit(solution)/shard_map/all_to_all | solution.py:464
  17.3 1.8 %smooth_block.1 = f32[32,4,128]{2,1,0:T(4,128)S(1)} custom-call(f32[32,8,128]{2,1,0:T(8,128)S(1)} %all_to_all.10.in_ref), custom_call_target="tpu_custom_call" | custom-call | tf_op jit(solution)/shard_map/smooth_block/pallas_call | solution.py:465
  19.1 9.2 %all_to_all.11.in_ref = f32[32,4,128]{2,1,0:T(4,128)S(1)} all-to-all(f32[32,4,128]{2,1,0:T(4,128)S(1)} %smooth_block.1), channel_id=1, replica_groups=mesh['cols'=8,'par'=4] {'cols','par'}, dimensions={0} | all-to-all | bytes 131072 | tf_op jit(solution)/shard_map/all_to_all | solution.py:473
  28.2 0.9 %collect_windows.1 = f32[3,1,8,256]{3,2,1,0:T(8,128)} custom-call(f32[32,4,128]{2,1,0:T(4,128)S(1)} %all_to_all.11.in_ref), custom_call_target="tpu_custom_call" | custom-call | tf_op jit(solution)/shard_map/collect_windows/pallas_call | solution.py:474

commit v5 on v4

--- a/solution.py
+++ b/solution.py
@@ -103,7 +103,7 @@
 
 LANES = 128
 SUBLANES = 8
-RAY_CHUNKS = 4
+RAY_CHUNKS = 2
 
 
 def device_index():
@@ -166,14 +166,54 @@
         copy.start()
 
     diagonal = lax.broadcasted_iota(jnp.int32, (rays, rays), 0) == lane_ids((rays, rays))
-    for copy in small[:2]:
+    for copy in small:
         copy.wait()
     for tile in range(tiles):
         live = lane_ids((1, rays)) < picks_ref[tile]
         weight = jnp.where(live, rmo_ref[tile : tile + 1, :].astype(jnp.float32), 0.0)
         column = jnp.sum(jnp.where(diagonal, weight, 0.0), axis=1, keepdims=True)
         weight_ref[tile] = jnp.broadcast_to(column, (rays, LANES))
-    sums = []
+
+    y_ids = lane_ids((1, rows_y))
+    place_in_packet = lax.rem(y_ids, width)
+
+    def packet_lane(values):
+        lane = jnp.zeros((1, rows_y), jnp.float32)
+        for q, value in enumerate(values):
+            lane = jnp.where(place_in_packet == q, value, lane)
+        return lane
+
+    factor_rows = [packet_lane([strength_ref[q] for q in range(params)])]
+    for p in range(params):
+        weights = [jnp.full((1, rows_y), couple_ref[p, q], jnp.float32) for q in range(params)]
+        whole = weights[0]
+        for weight in weights[1:]:
+            whole = whole + weight
+        factor_rows.append(packet_lane([weight / whole for weight in weights]))
+
+    first_depth, lane_first, place_rows, first_half = [], [], [], []
+    for tile in range(tiles):
+        first_depth.append(anchor_ref[tile, 0])
+        first = bounds_ref[lax.axis_index("cols")] + anchor_ref[tile, 1]
+        first_x = first // rows_y
+        first_y = first - first_x * rows_y
+        first_half.append(first_y // LANES)
+        lane_first.append(first_y - first_half[tile] * LANES)
+        at_x = first_x + (y_ids < first_y).astype(jnp.int32)
+        place_rows.append((at_x * devices + first_depth[tile]).astype(jnp.float32))
+    notes = jnp.concatenate(
+        [jnp.zeros((3 * width, rows_y), jnp.float32)]
+        + place_rows
+        + factor_rows
+        + [jnp.zeros((devices - 3 * width - tiles - params - 1, rows_y), jnp.float32)],
+        axis=0,
+    )
+    dip = dip_ref[0].astype(jnp.float32)
+    count = LANES // width
+    for device in range(devices):
+        out_ref[device] = roll_lanes(dip, width - device * width)[:, :LANES]
+
+    parts = [[[None] * tiles for _ in range(params)] for _ in range(halves)]
     for tile in range(tiles):
         total = jnp.zeros((params, tile_depth, tile_columns), jnp.float32)
         for ray in range(rays):
@@ -181,54 +221,18 @@
                 large[tile][ray // chunk].wait()
             weight = weight_ref[tile, ray : ray + 1, :]
             total = total + weight[None] * sens_ref[tile, ray].astype(jnp.float32)
-        sums.append(total)
-    for copy in small[2:]:
-        copy.wait()
-
-    parts = [[[None] * tiles for _ in range(params)] for _ in range(halves)]
-    x_rows, depth_rows = [], []
-    y_ids = lane_ids((1, rows_y))
-    for tile in range(tiles):
-        depth_first = anchor_ref[tile, 0]
-        first = bounds_ref[lax.axis_index("cols")] + anchor_ref[tile, 1]
-        first_x = first // rows_y
-        first_y = first - first_x * rows_y
-        half_of = first_y // LANES
-        lane_first = first_y - half_of * LANES
-        past = lane_ids((1, LANES)) >= lane_first
+        past = lane_ids((1, LANES)) >= lane_first[tile]
         for param in range(params):
-            turned = pltpu.roll(sums[tile][param], lax.rem(depth_first, tile_depth), 0)
-            turned = pltpu.roll(turned, lane_first, 1)
+            turned = pltpu.roll(total[param], lax.rem(first_depth[tile], tile_depth), 0)
+            turned = pltpu.roll(turned, lane_first[tile], 1)
             for half in range(halves):
-                after = lax.rem(half_of + 1, halves)
+                after = lax.rem(first_half[tile] + 1, halves)
                 kept = jnp.logical_or(
-                    jnp.logical_and(past, half_of == half),
+                    jnp.logical_and(past, first_half[tile] == half),
                     jnp.logical_and(jnp.logical_not(past), after == half),
                 )
                 parts[half][param][tile] = jnp.where(kept, turned, 0.0)
-        x_rows.append((first_x + (y_ids < first_y).astype(jnp.int32)).astype(jnp.float32))
-        depth_rows.append(jnp.full((1, rows_y), depth_first, jnp.int32).astype(jnp.float32))
-    place_in_packet = lax.rem(y_ids, width)
-
-    def packet_lane(values):
-        lane = jnp.zeros((1, rows_y), jnp.float32)
-        for q, value in enumerate(values):
-            lane = jnp.where(place_in_packet == q, value, lane)
-        return lane
-
-    factor_rows = [packet_lane([strength_ref[q] for q in range(params)])]
-    for p in range(params):
-        weights = [jnp.full((1, rows_y), couple_ref[p, q], jnp.float32) for q in range(params)]
-        whole = weights[0]
-        for weight in weights[1:]:
-            whole = whole + weight
-        factor_rows.append(packet_lane([weight / whole for weight in weights]))
-    notes = jnp.concatenate(
-        [jnp.zeros((3 * width, rows_y), jnp.float32)] + x_rows + depth_rows + factor_rows, axis=0
-    )
-    dip = dip_ref[0].astype(jnp.float32)
     in_window = lane_ids((rows_x, LANES)) < 3 * width
-    count = LANES // width
     for half in range(halves):
         rows = [notes[:, half * LANES : (half + 1) * LANES]]
         for param in range(params):
@@ -236,8 +240,9 @@
         turned = jnp.transpose(jnp.concatenate(rows, axis=0))
         for place in range(count):
             device = half * count + place
-            window = roll_lanes(dip, width - device * width)[:, :LANES]
-            out_ref[device] = jnp.where(in_window, window, turned[place * width : (place + 1) * width])
+            out_ref[device] = jnp.where(
+                in_window, out_ref[device], turned[place * width : (place + 1) * width]
+            )
 
 
 def smooth_kernel(in_ref, out_ref, *, params, tiles, rows_x, rows_y):
@@ -247,32 +252,30 @@
     rows = 3 * width
     side = rows
     lane = lane_ids((width, LANES))
-    z = lane % depth
-    low = z < depth // 2
-    z_float = z.astype(jnp.float32)
-
-    def add_source(source, field):
+    low = lane % depth < depth // 2
+    in_tile = (lane % (depth // 2)).astype(jnp.float32)
+    zero = jnp.zeros((width, LANES), jnp.float32)
+    stays = [zero] * rows_x
+    moves = [zero] * rows_x
+    for source in range(depth):
         message = in_ref[source]
-        swapped = jnp.where(low, roll_lanes(message, -(depth // 2)), roll_lanes(message, depth // 2))
-        field = list(field)
-        for tile in range(tiles):
-            own = low if tile == 0 else jnp.logical_not(low)
-            values = jnp.where(own, message, swapped)
-            at_x = jnp.broadcast_to(message[:, side + tile : side + tile + 1], (width, LANES))
-            first_z = jnp.broadcast_to(
-                message[:, side + tiles + tile : side + tiles + tile + 1], (width, LANES)
-            )
-            behind = z_float - first_z
-            inside = jnp.logical_and(behind >= 0.0, behind < float(depth // 2))
-            at_x = jnp.where(inside, at_x, -1.0)
-            for x in range(rows_x):
-                field[x] = field[x] + jnp.where(at_x == float(x), values, 0.0)
-        return tuple(field)
-
-    zero = jnp.zeros((width, LANES), jnp.float32)
-    field = (zero,) * rows_x
-    for source in range(depth):
-        field = add_source(source, field)
+        at = [
+            jnp.broadcast_to(message[:, side + tile : side + tile + 1], (width, LANES))
+            for tile in range(tiles)
+        ]
+        at = jnp.where(low, at[0], at[1])
+        at_x = jnp.floor(at * (1.0 / depth))
+        below_first = in_tile < at - at_x * depth
+        stay = jnp.logical_xor(low, below_first)
+        at_stay = jnp.where(stay, at_x, -1.0)
+        at_move = jnp.where(stay, -1.0, at_x)
+        for x in range(rows_x):
+            stays[x] = stays[x] + jnp.where(at_stay == float(x), message, 0.0)
+            moves[x] = moves[x] + jnp.where(at_move == float(x), message, 0.0)
+    field = [
+        stay + jnp.where(low, roll_lanes(move, -(depth // 2)), roll_lanes(move, depth // 2))
+        for stay, move in zip(stays, moves)
+    ]
 
     block = lane // depth
     current = []
@@ -281,13 +284,13 @@
         for half in range(halves):
             centre = zero
             for group in range(groups):
-                moved = roll_lanes(field[half * groups + group], depth * (group - param - 1))
+                moved = roll_lanes(field[group * halves + half], depth * (group - param - 1))
                 centre = jnp.where(block == group, moved, centre)
             current[param].append(jnp.concatenate([zero, centre, zero], axis=0))
 
     dip = []
     for half in range(halves):
-        layers = [in_ref[:, half * groups + group, :] for group in range(groups)]
+        layers = [in_ref[:, group * halves + half, :] for group in range(groups)]
         dip.append(jnp.transpose(jnp.concatenate(layers, axis=0))[:rows])
 
     lanes = lane_ids((rows, LANES))
@@ -295,75 +298,66 @@
     block = lanes // depth
     first = block == 0
     last = block == groups - 1
-    top = z == 0
-    bottom = z == depth - 1
     y = device_index() * width - width + lax.broadcasted_iota(jnp.int32, (rows, LANES), 0)
     in_grid = jnp.logical_and(y >= 0, y < rows_y)
 
-    def from_next_x(values):
-        moved = [roll_lanes(v, -depth) for v in values]
-        return [
-            jnp.where(last, moved[h + 1] if h + 1 < halves else 0.0, moved[h]) for h in range(halves)
-        ]
-
-    def from_prev_x(values):
-        moved = [roll_lanes(v, depth) for v in values]
-        return [jnp.where(first, moved[h - 1] if h > 0 else 0.0, moved[h]) for h in range(halves)]
-
-    def from_next_y(values):
-        return [pltpu.roll(v, rows - 1, 0) for v in values]
-
-    def from_prev_y(values):
-        return [pltpu.roll(v, 1, 0) for v in values]
-
-    def masks(values):
-        return [(v < -0.5, v > 0.5) for v in values]
-
-    tilt_x = [jnp.where(d < 2.5, -1.0, jnp.where(d > 5.5, 1.0, 0.0)) for d in dip]
-    tilt_y = [d - 3.0 * (t + 1.0) - 1.0 for d, t in zip(dip, tilt_x)]
-    to_west = masks(from_prev_x(tilt_x))
-    to_east = masks(from_next_x(tilt_x))
-    to_south = masks(from_prev_y(tilt_y))
-    to_north = masks(from_next_y(tilt_y))
-
     def factor(lane, q):
-        at = side + 2 * tiles + lane
+        at = side + tiles + lane
         return jnp.broadcast_to(in_ref[0, q : q + 1, at : at + 1], (rows, LANES))
 
     strengths = [factor(0, q) for q in range(params)]
+    keeps = [1.0 - 4.0 * strength for strength in strengths]
     mixing = [
         [jnp.where(in_grid, factor(p + 1, q), 0.0) for q in range(params)] for p in range(params)
     ]
+
+    def codes(tilt, inside=True):
+        level = jnp.where(jnp.abs(tilt) < 0.5, 1.0, 0.0)
+        above = jnp.where(jnp.logical_and(tilt < -0.5, z > 0), 1.0, 0.0)
+        below = jnp.where(jnp.logical_and(tilt > 0.5, z < depth - 1), 1.0, 0.0)
+        return [jnp.where(inside, weight, 0.0) for weight in (level, above, below)]
+
+    def candidates(values, shift):
+        return [roll_lanes(values, shift + step) for step in (0, 1, -1)]
+
+    def chosen(values, weights):
+        total = values[0] * weights[0]
+        for value, weight in zip(values[1:], weights[1:]):
+            total = total + value * weight
+        return total
+
+    def next_y(values):
+        return pltpu.roll(values, rows - 1, 0)
+
+    def prev_y(values):
+        return pltpu.roll(values, 1, 0)
+
+    east, west, north, south = [], [], [], []
+    for half in range(halves):
+        tilt_x = jnp.where(dip[half] < 2.5, -1.0, jnp.where(dip[half] > 5.5, 1.0, 0.0))
+        tilt_y = dip[half] - 3.0 * tilt_x - 4.0
+        east.append(codes(tilt_x, jnp.logical_or(half + 1 < halves, jnp.logical_not(last))))
+        west.append(codes(-tilt_x, jnp.logical_or(half > 0, jnp.logical_not(first))))
+        north.append(codes(prev_y(tilt_y)))
+        south.append(codes(-next_y(tilt_y)))
 
     for _ in range(PASSES):
         smooth = []
         for q in range(params):
             u = current[q]
-            above = [jnp.where(top, 0.0, roll_lanes(v, 1)) for v in u]
-            below = [jnp.where(bottom, 0.0, roll_lanes(v, -1)) for v in u]
-
-            def plus(tilts):
-                return [
-                    jnp.where(neg, a, jnp.where(pos, b, v))
-                    for (neg, pos), a, v, b in zip(tilts, above, u, below)
-                ]
-
-            def minus(tilts):
-                return [
-                    jnp.where(neg, b, jnp.where(pos, a, v))
-                    for (neg, pos), a, v, b in zip(tilts, above, u, below)
-                ]
-
-            east = from_next_x(plus(to_west))
-            west = from_prev_x(minus(to_east))
-            north = from_next_y(plus(to_south))
-            south = from_prev_y(minus(to_north))
-            smooth.append(
-                [
-                    v + strengths[q] * (e + w + n + s - 4.0 * v)
-                    for v, e, w, n, s in zip(u, east, west, north, south)
-                ]
-            )
+            near = [candidates(values, 0) for values in u]
+            row = []
+            for half in range(halves):
+                ahead = near[half + 1] if half + 1 < halves else candidates(u[0], -depth)
+                behind = near[half - 1] if half > 0 else candidates(u[-1], depth)
+                total = (
+                    chosen(ahead, east[half])
+                    + chosen(behind, west[half])
+                    + next_y(chosen(near[half], north[half]))
+                    + prev_y(chosen(near[half], south[half]))
+                )
+                row.append(keeps[q] * u[half] + strengths[q] * total)
+            smooth.append(row)
         current = []
         for p in range(params):
             mixed = []
@@ -408,7 +402,11 @@
                 totals[param][column] = totals[param][column] + jnp.where(inside, placed, 0.0)
     for param in range(params):
         for column in range(rows_y // LANES):
-            out_ref[param, 0, :, column * LANES : (column + 1) * LANES] = totals[param][column]
+            for x in range(rows_x):
+                row = (x % halves) * groups + x // halves
+                out_ref[param, 0, x : x + 1, column * LANES : (column + 1) * LANES] = totals[param][
+                    column
+                ][row : row + 1]
 
 
 def fits(sensitivity, dip_class, devices):
@@ -425,7 +423,7 @@
         and tiles == 2
         and tiles * tile_depth == depth
         and (params + 1) * depth == LANES
-        and 3 * SUBLANES + 2 * tiles + params + 1 == depth
+        and 3 * SUBLANES + tiles + params + 1 <= depth
         and rays % RAY_CHUNKS == 0
         and rows_x * params * (SUBLANES + 2 * PASSES) <= 4 * LANES
     )

time: 29.3 us -> 28.9 us (0.986)
  Pallas kernels: 4.57 us -> 4.14 us
where the time goes in v5:
time: 28.9 us; the launch traced here: 28.7 us
  blocking collectives  24.5 us (85%)
  Pallas kernels  4.14 us (14%)
    all_to_all x1, blocking collectives, shards_by_y(): received = lax.all_to_all(sent, ('cols', 'par'), 0, 0)  15.3 us
    all_to_all x1, blocking collectives, shards_by_y(): windows = lax.all_to_all(layers, ('cols', 'par'), 0, 0)  9.18 us
    pallas_call x1, Pallas kernels, shards_by_y(): pl.pallas_call(source_kernel, out_shape=pltpu.VMEM((devices, width, LANES...  1.74 us
    pallas_call x1, Pallas kernels, shards_by_y(): pl.pallas_call(functools.partial(smooth_kernel, params=params, tiles=tile...  1.54 us
    pallas_call x1, Pallas kernels, shards_by_y(): pl.pallas_call(functools.partial(collect_kernel, width=width), out_shape=...  0.86 us

profile of v5, /device:TPU:0, one launch (start us, length us, event | category | flops | bytes accessed | tf_op | source)
XLA Modules:
  0.0 28.7 jit_solution(1559440392135771461)
XLA Ops:
  0.0 1.7 %sum_rays.1 = f32[32,8,128]{2,1,0:T(8,128)S(1)} custom-call(s32[9]{0:T(128)} %bounds_hbm.1, s32[2,2]{1,0:T(2,128)} %anchor_hbm.1, s32[2]{0:T(128)} %picks_hbm.1, bf16[2,64]{1,0:T(2,128)(2,1)} %rmo_hbm.1, bf16[2,64,3,16,128]{4,3,2,1,0:T(8,128)(2,1)} %sens_hbm.1, s32[1,8,256]{2,1,0:T(8,128)} %dip_hbm.1, f32[3]{0:T(128)} %strength_hbm.1, f32[3,3]{1,0:T(4,128)} %couple_hbm.1), custom_call_target="tpu_custom_call" | custom-call | tf_op jit(solution)/shard_map/sum_rays/pallas_call | solution.py:448
  1.8 15.3 %all_to_all.10.in_ref = f32[32,8,128]{2,1,0:T(8,128)S(1)} all-to-all(f32[32,8,128]{2,1,0:T(8,128)S(1)} %sum_rays.1), channel_id=1, replica_groups=mesh['cols'=8,'par'=4] {'cols','par'}, dimensions={0} | all-to-all | bytes 262144 | tf_op jit(solution)/shard_map/all_to_all | solution.py:462
  17.1 1.5 %smooth_block.1 = f32[32,4,128]{2,1,0:T(4,128)S(1)} custom-call(f32[32,8,128]{2,1,0:T(8,128)S(1)} %all_to_all.10.in_ref), custom_call_target="tpu_custom_call" | custom-call | tf_op jit(solution)/shard_map/smooth_block/pallas_call | solution.py:463
  18.6 9.2 %all_to_all.11.in_ref = f32[32,4,128]{2,1,0:T(4,128)S(1)} all-to-all(f32[32,4,128]{2,1,0:T(4,128)S(1)} %smooth_block.1), channel_id=1, replica_groups=mesh['cols'=8,'par'=4] {'cols','par'}, dimensions={0} | all-to-all | bytes 131072 | tf_op jit(solution)/shard_map/all_to_all | solution.py:471
  27.8 0.9 %collect_windows.1 = f32[3,1,8,256]{3,2,1,0:T(8,128)} custom-call(f32[32,4,128]{2,1,0:T(4,128)S(1)} %all_to_all.11.in_ref), custom_call_target="tpu_custom_call" | custom-call | tf_op jit(solution)/shard_map/collect_windows/pallas_call | solution.py:472

commit v6 on v5

--- a/solution.py
+++ b/solution.py
@@ -168,9 +168,10 @@
     diagonal = lax.broadcasted_iota(jnp.int32, (rays, rays), 0) == lane_ids((rays, rays))
     for copy in small:
         copy.wait()
+    residuals = rmo_ref[...].astype(jnp.float32)
     for tile in range(tiles):
         live = lane_ids((1, rays)) < picks_ref[tile]
-        weight = jnp.where(live, rmo_ref[tile : tile + 1, :].astype(jnp.float32), 0.0)
+        weight = jnp.where(live, residuals[tile : tile + 1], 0.0)
         column = jnp.sum(jnp.where(diagonal, weight, 0.0), axis=1, keepdims=True)
         weight_ref[tile] = jnp.broadcast_to(column, (rays, LANES))
 
@@ -272,11 +273,6 @@
         for x in range(rows_x):
             stays[x] = stays[x] + jnp.where(at_stay == float(x), message, 0.0)
             moves[x] = moves[x] + jnp.where(at_move == float(x), message, 0.0)
-    field = [
-        stay + jnp.where(low, roll_lanes(move, -(depth // 2)), roll_lanes(move, depth // 2))
-        for stay, move in zip(stays, moves)
-    ]
-
     block = lane // depth
     current = []
     for param in range(params):
@@ -284,9 +280,15 @@
         for half in range(halves):
             centre = zero
             for group in range(groups):
-                moved = roll_lanes(field[group * halves + half], depth * (group - param - 1))
-                centre = jnp.where(block == group, moved, centre)
-            current[param].append(jnp.concatenate([zero, centre, zero], axis=0))
+                x = group * halves + half
+                shift = depth * (group - param - 1)
+                moved = jnp.where(
+                    low,
+                    roll_lanes(moves[x], shift - depth // 2),
+                    roll_lanes(moves[x], shift + depth // 2),
+                )
+                centre = jnp.where(block == group, roll_lanes(stays[x], shift) + moved, centre)
+            current[param].append([None, centre, None])
 
     dip = []
     for half in range(halves):
@@ -298,39 +300,71 @@
     block = lanes // depth
     first = block == 0
     last = block == groups - 1
-    y = device_index() * width - width + lax.broadcasted_iota(jnp.int32, (rows, LANES), 0)
-    in_grid = jnp.logical_and(y >= 0, y < rows_y)
+    bands = range(3)
+    own = device_index()
+    in_grid = [
+        jnp.where(own > 0, 1.0, 0.0),
+        1.0,
+        jnp.where(own < rows_y // width - 1, 1.0, 0.0),
+    ]
+
+    def by_band(values):
+        return [values[band * width : (band + 1) * width] for band in bands]
 
     def factor(lane, q):
         at = side + tiles + lane
-        return jnp.broadcast_to(in_ref[0, q : q + 1, at : at + 1], (rows, LANES))
+        return jnp.broadcast_to(in_ref[0, q : q + 1, at : at + 1], (width, LANES))
 
     strengths = [factor(0, q) for q in range(params)]
-    keeps = [1.0 - 4.0 * strength for strength in strengths]
+    keeps = [1.0 / strength - 4.0 for strength in strengths]
     mixing = [
-        [jnp.where(in_grid, factor(p + 1, q), 0.0) for q in range(params)] for p in range(params)
+        [
+            [factor(p + 1, q) * strengths[q] * in_grid[band] for band in bands]
+            for q in range(params)
+        ]
+        for p in range(params)
     ]
 
     def codes(tilt, inside=True):
         level = jnp.where(jnp.abs(tilt) < 0.5, 1.0, 0.0)
         above = jnp.where(jnp.logical_and(tilt < -0.5, z > 0), 1.0, 0.0)
         below = jnp.where(jnp.logical_and(tilt > 0.5, z < depth - 1), 1.0, 0.0)
-        return [jnp.where(inside, weight, 0.0) for weight in (level, above, below)]
+        weights = [by_band(jnp.where(inside, weight, 0.0)) for weight in (level, above, below)]
+        return list(zip(*weights))
+
+    def chosen(weights, many):
+        results = []
+        for values in many:
+            if values is None:
+                results.append(None)
+                continue
+            total = values[0] * weights[0]
+            for value, weight in zip(values[1:], weights[1:]):
+                total = total + value * weight
+            results.append(total)
+        return results
 
     def candidates(values, shift):
+        if values is None:
+            return None
         return [roll_lanes(values, shift + step) for step in (0, 1, -1)]
 
-    def chosen(values, weights):
-        total = values[0] * weights[0]
-        for value, weight in zip(values[1:], weights[1:]):
-            total = total + value * weight
+    row_ids = lax.broadcasted_iota(jnp.int32, (width, LANES), 0)
+
+    def moved_y(here, there, step):
+        if here is None and there is None:
+            return None
+        parts = [
+            0.0 if values is None else pltpu.roll(values, step % width, 0) for values in (here, there)
+        ]
+        return jnp.where(row_ids == (width - 1 if step < 0 else 0), parts[1], parts[0])
+
+    def added(terms):
+        terms = [term for term in terms if term is not None]
+        total = terms[0] if terms else None
+        for term in terms[1:]:
+            total = total + term
         return total
-
-    def next_y(values):
-        return pltpu.roll(values, rows - 1, 0)
-
-    def prev_y(values):
-        return pltpu.roll(values, 1, 0)
 
     east, west, north, south = [], [], [], []
     for half in range(halves):
@@ -338,35 +372,86 @@
         tilt_y = dip[half] - 3.0 * tilt_x - 4.0
         east.append(codes(tilt_x, jnp.logical_or(half + 1 < halves, jnp.logical_not(last))))
         west.append(codes(-tilt_x, jnp.logical_or(half > 0, jnp.logical_not(first))))
-        north.append(codes(prev_y(tilt_y)))
-        south.append(codes(-next_y(tilt_y)))
-
-    for _ in range(PASSES):
-        smooth = []
-        for q in range(params):
-            u = current[q]
-            near = [candidates(values, 0) for values in u]
-            row = []
+        north.append(codes(pltpu.roll(tilt_y, 1, 0)))
+        south.append(codes(-pltpu.roll(tilt_y, rows - 1, 0)))
+
+    def prepare(u, half):
+        return [
+            (
+                v,
+                candidates(v, 0),
+                candidates(v, -depth) if half == 0 else None,
+                candidates(v, depth) if half == halves - 1 else None,
+            )
+            for v in u
+        ]
+
+    ready = {
+        (half, band): prepare([current[p][half][band] for p in range(params)], half)
+        for band in bands
+        for half in range(halves)
+    }
+    def in_turn(weight, earlier):
+        return weight if earlier is None else jnp.maximum(weight, jnp.minimum(earlier, -1e30))
+
+    for step in range(PASSES):
+        turned_south, turned_north = {}, {}
+        following = {}
+        done = None
+
+        def to_south(half, band):
+            if (half, band) not in turned_south:
+                many = [item[1] for item in ready[half, band]]
+                turned_south[half, band] = chosen(north[half][band], many)
+            return turned_south[half, band]
+
+        def to_north(half, band):
+            if (half, band) not in turned_north:
+                many = [item[1] for item in ready[half, band]]
+                turned_north[half, band] = chosen(south[half][band], many)
+            return turned_north[half, band]
+
+        for band in bands:
             for half in range(halves):
-                ahead = near[half + 1] if half + 1 < halves else candidates(u[0], -depth)
-                behind = near[half - 1] if half > 0 else candidates(u[-1], depth)
-                total = (
-                    chosen(ahead, east[half])
-                    + chosen(behind, west[half])
-                    + next_y(chosen(near[half], north[half]))
-                    + prev_y(chosen(near[half], south[half]))
-                )
-                row.append(keeps[q] * u[half] + strengths[q] * total)
-            smooth.append(row)
-        current = []
-        for p in range(params):
-            mixed = []
-            for half in range(halves):
-                value = mixing[p][0] * smooth[0][half]
-                for q in range(1, params):
-                    value = value + mixing[p][q] * smooth[q][half]
-                mixed.append(value)
-            current.append(mixed)
+                if half + 1 < halves:
+                    ahead = [item[1] for item in ready[half + 1, band]]
+                else:
+                    ahead = [item[2] for item in ready[0, band]]
+                if half > 0:
+                    behind = [item[1] for item in ready[half - 1, band]]
+                else:
+                    behind = [item[3] for item in ready[halves - 1, band]]
+                level, above, below = east[half][band]
+                to_west = chosen((in_turn(level, done), above, below), ahead)
+                to_east = chosen(west[half][band], behind)
+                sums = []
+                for q in range(params):
+                    u = ready[half, band][q][0]
+                    upper = to_south(half, band + 1)[q] if band + 1 < len(bands) else None
+                    lower = to_north(half, band - 1)[q] if band > 0 else None
+                    sums.append(
+                        added(
+                            [
+                                to_west[q],
+                                to_east[q],
+                                None if u is None else keeps[q] * u,
+                                moved_y(to_south(half, band)[q], upper, -1),
+                                moved_y(to_north(half, band)[q], lower, 1),
+                            ]
+                        )
+                    )
+                new = [
+                    added([mixing[p][q][band] * sums[q] for q in range(params)])
+                    for p in range(params)
+                ]
+                done = new[0]
+                if step + 1 < PASSES:
+                    following[half, band] = prepare(new, half)
+                else:
+                    for p in range(params):
+                        current[p][half][band] = new[p]
+        ready = following
+    current = [[jnp.concatenate(bands_of, axis=0) for bands_of in u] for u in current]
 
     pieces = []
     for half in range(halves):

time: 28.9 us -> 28.6 us (0.990)
  no operation moved by 1% of the time
where the time goes in v6:
time: 28.6 us; the launch traced here: 28.4 us
  blocking collectives  24.5 us (86%)
  Pallas kernels  3.91 us (14%)
    all_to_all x1, blocking collectives, shards_by_y(): received = lax.all_to_all(sent, ('cols', 'par'), 0, 0)  15.3 us
    all_to_all x1, blocking collectives, shards_by_y(): windows = lax.all_to_all(layers, ('cols', 'par'), 0, 0)  9.18 us
    pallas_call x1, Pallas kernels, shards_by_y(): pl.pallas_call(source_kernel, out_shape=pltpu.VMEM((devices, width, LANES...  1.74 us
    pallas_call x1, Pallas kernels, shards_by_y(): pl.pallas_call(functools.partial(smooth_kernel, params=params, tiles=tile...  1.3 us
    pallas_call x1, Pallas kernels, shards_by_y(): pl.pallas_call(functools.partial(collect_kernel, width=width), out_shape=...  0.86 us

profile of v6, /device:TPU:0, one launch (start us, length us, event | category | flops | bytes accessed | tf_op | source)
XLA Modules:
  0.0 28.4 jit_solution(16391012169784545970)
XLA Ops:
  0.0 1.7 %sum_rays.1 = f32[32,8,128]{2,1,0:T(8,128)S(1)} custom-call(s32[9]{0:T(128)} %bounds_hbm.1, s32[2,2]{1,0:T(2,128)} %anchor_hbm.1, s32[2]{0:T(128)} %picks_hbm.1, bf16[2,64]{1,0:T(2,128)(2,1)} %rmo_hbm.1, bf16[2,64,3,16,128]{4,3,2,1,0:T(8,128)(2,1)} %sens_hbm.1, s32[1,8,256]{2,1,0:T(8,128)} %dip_hbm.1, f32[3]{0:T(128)} %strength_hbm.1, f32[3,3]{1,0:T(4,128)} %couple_hbm.1), custom_call_target="tpu_custom_call" | custom-call | tf_op jit(solution)/shard_map/sum_rays/pallas_call | solution.py:533
  1.8 15.3 %all_to_all.10.in_ref = f32[32,8,128]{2,1,0:T(8,128)S(1)} all-to-all(f32[32,8,128]{2,1,0:T(8,128)S(1)} %sum_rays.1), channel_id=1, replica_groups=mesh['cols'=8,'par'=4] {'cols','par'}, dimensions={0} | all-to-all | bytes 262144 | tf_op jit(solution)/shard_map/all_to_all | solution.py:547
  17.1 1.3 %smooth_block.1 = f32[32,4,128]{2,1,0:T(4,128)S(1)} custom-call(f32[32,8,128]{2,1,0:T(8,128)S(1)} %all_to_all.10.in_ref), custom_call_target="tpu_custom_call" | custom-call | tf_op jit(solution)/shard_map/smooth_block/pallas_call | solution.py:548
  18.4 9.2 %all_to_all.11.in_ref = f32[32,4,128]{2,1,0:T(4,128)S(1)} all-to-all(f32[32,4,128]{2,1,0:T(4,128)S(1)} %smooth_block.1), channel_id=1, replica_groups=mesh['cols'=8,'par'=4] {'cols','par'}, dimensions={0} | all-to-all | bytes 131072 | tf_op jit(solution)/shard_map/all_to_all | solution.py:556
  27.6 0.9 %collect_windows.1 = f32[3,1,8,256]{3,2,1,0:T(8,128)} custom-call(f32[32,4,128]{2,1,0:T(4,128)S(1)} %all_to_all.11.in_ref), custom_call_target="tpu_custom_call" | custom-call | tf_op jit(solution)/shard_map/collect_windows/pallas_call | solution.py:557

commit v7 on v6

--- a/solution.py
+++ b/solution.py
@@ -106,8 +106,8 @@
 RAY_CHUNKS = 2
 
 
-def device_index():
-    return lax.axis_index("cols") * lax.axis_size("par") + lax.axis_index("par")
+def block_index():
+    return lax.axis_index("par") * lax.axis_size("cols") + lax.axis_index("cols")
 
 
 def lane_ids(shape):
@@ -246,7 +246,7 @@
             )
 
 
-def smooth_kernel(in_ref, out_ref, *, params, tiles, rows_x, rows_y):
+def smooth_kernel(in_ref, out_ref, layer_ref, *, params, tiles, replicas, rows_x, rows_y):
     depth, width, _ = in_ref.shape
     groups = LANES // depth
     halves = rows_x // groups
@@ -292,8 +292,13 @@
 
     dip = []
     for half in range(halves):
-        layers = [in_ref[:, group * halves + half, :] for group in range(groups)]
-        dip.append(jnp.transpose(jnp.concatenate(layers, axis=0))[:rows])
+        columns = depth // replicas
+        for group in range(groups):
+            for replica in range(replicas):
+                layer_ref[half, pl.ds(group * depth + replica, columns, replicas), :] = in_ref[
+                    replica * columns : (replica + 1) * columns, group * halves + half, :
+                ]
+        dip.append(jnp.transpose(layer_ref[half])[:rows])
 
     lanes = lane_ids((rows, LANES))
     z = lanes % depth
@@ -301,7 +306,7 @@
     first = block == 0
     last = block == groups - 1
     bands = range(3)
-    own = device_index()
+    own = block_index()
     in_grid = [
         jnp.where(own > 0, 1.0, 0.0),
         1.0,
@@ -459,9 +464,12 @@
             pieces.append(current[p][half][width - PASSES : 2 * width + PASSES])
     used = halves * params * (width + 2 * PASSES)
     pieces.append(jnp.zeros((LANES - used, LANES), jnp.float32))
-    turned = jnp.transpose(jnp.concatenate(pieces, axis=0))
+    layer_ref[0] = jnp.transpose(jnp.concatenate(pieces, axis=0))
     for group in range(groups):
-        out_ref[:, group, :] = turned[group * depth : (group + 1) * depth]
+        for replica in range(replicas):
+            out_ref[replica * columns : (replica + 1) * columns, group, :] = layer_ref[
+                0, pl.ds(group * depth + replica, columns, replicas), :
+            ]
 
 
 def collect_kernel(in_ref, out_ref, *, width):
@@ -519,7 +527,8 @@
 ):
     tiles, rays, params, _, _ = sensitivity.shape
     _, rows_x, rows_y = dip_class.shape
-    devices = lax.axis_size("cols") * lax.axis_size("par")
+    replicas = lax.axis_size("par")
+    devices = lax.axis_size("cols") * replicas
     width = rows_y // devices
     groups = LANES // devices
     hbm = pl.BlockSpec(memory_space=pltpu.HBM)
@@ -544,16 +553,24 @@
         compiler_params=pltpu.CompilerParams(vmem_limit_bytes=32 << 20),
         name="sum_rays",
     )(*(pltpu.with_memory_space_constraint(array, pltpu.HBM) for array in arguments))
-    received = lax.all_to_all(sent, ("cols", "par"), 0, 0)
+    received = lax.all_to_all(sent, ("par", "cols"), 0, 0)
     layers = pl.pallas_call(
-        functools.partial(smooth_kernel, params=params, tiles=tiles, rows_x=rows_x, rows_y=rows_y),
+        functools.partial(
+            smooth_kernel,
+            params=params,
+            tiles=tiles,
+            replicas=replicas,
+            rows_x=rows_x,
+            rows_y=rows_y,
+        ),
         out_shape=jax.ShapeDtypeStruct((devices, groups, LANES), jnp.float32),
         in_specs=[vmem],
         out_specs=vmem,
+        scratch_shapes=[pltpu.VMEM((rows_x // groups, LANES, LANES), jnp.float32)],
         compiler_params=pltpu.CompilerParams(vmem_limit_bytes=32 << 20),
         name="smooth_block",
     )(received)
-    windows = lax.all_to_all(layers, ("cols", "par"), 0, 0)
+    windows = lax.all_to_all(layers, ("par", "cols"), 0, 0)
     return pl.pallas_call(
         functools.partial(collect_kernel, width=width),
         out_shape=jax.ShapeDtypeStruct((params, 1, rows_x, rows_y), jnp.float32),

time: 28.6 us -> 28.5 us (level)
  no operation moved by 1% of the time
where the time goes in v7:
time: 28.5 us; the launch traced here: 28.3 us
  blocking collectives  24.4 us (86%)
  Pallas kernels  3.94 us (14%)
    all_to_all x1, blocking collectives, shards_by_y(): received = lax.all_to_all(sent, ('par', 'cols'), 0, 0)  14.8 us
    all_to_all x1, blocking collectives, shards_by_y(): windows = lax.all_to_all(layers, ('par', 'cols'), 0, 0)  9.54 us
    pallas_call x1, Pallas kernels, shards_by_y(): pl.pallas_call(source_kernel, out_shape=pltpu.VMEM((devices, width, LANES...  1.74 us
    pallas_call x1, Pallas kernels, shards_by_y(): pl.pallas_call(functools.partial(smooth_kernel, params=params, tiles=tile...  1.34 us
    pallas_call x1, Pallas kernels, shards_by_y(): pl.pallas_call(functools.partial(collect_kernel, width=width), out_shape=...  0.86 us

profile of v7, /device:TPU:0, one launch (start us, length us, event | category | flops | bytes accessed | tf_op | source)
XLA Modules:
  0.0 28.3 jit_solution(4943910908748713773)
XLA Ops:
  0.0 1.7 %sum_rays.1 = f32[32,8,128]{2,1,0:T(8,128)S(1)} custom-call(s32[9]{0:T(128)} %bounds_hbm.1, s32[2,2]{1,0:T(2,128)} %anchor_hbm.1, s32[2]{0:T(128)} %picks_hbm.1, bf16[2,64]{1,0:T(2,128)(2,1)} %rmo_hbm.1, bf16[2,64,3,16,128]{4,3,2,1,0:T(8,128)(2,1)} %sens_hbm.1, s32[1,8,256]{2,1,0:T(8,128)} %dip_hbm.1, f32[3]{0:T(128)} %strength_hbm.1, f32[3,3]{1,0:T(4,128)} %couple_hbm.1), custom_call_target="tpu_custom_call" | custom-call | tf_op jit(solution)/shard_map/sum_rays/pallas_call | solution.py:542
  1.8 14.8 %all_to_all.10.in_ref = f32[32,8,128]{2,1,0:T(8,128)S(1)} all-to-all(f32[32,8,128]{2,1,0:T(8,128)S(1)} %sum_rays.1), channel_id=1, replica_groups=mesh['cols'=8,'par'=4] {'par','cols'}, dimensions={0} | all-to-all | bytes 262144 | tf_op jit(solution)/shard_map/all_to_all | solution.py:556
  16.6 1.3 %smooth_block.1 = f32[32,4,128]{2,1,0:T(4,128)S(1)} custom-call(f32[32,8,128]{2,1,0:T(8,128)S(1)} %all_to_all.10.in_ref), custom_call_target="tpu_custom_call" | custom-call | tf_op jit(solution)/shard_map/smooth_block/pallas_call | solution.py:557
  17.9 9.5 %all_to_all.11.in_ref = f32[32,4,128]{2,1,0:T(4,128)S(1)} all-to-all(f32[32,4,128]{2,1,0:T(4,128)S(1)} %smooth_block.1), channel_id=1, replica_groups=mesh['cols'=8,'par'=4] {'par','cols'}, dimensions={0} | all-to-all | bytes 131072 | tf_op jit(solution)/shard_map/all_to_all | solution.py:573
  27.5 0.9 %collect_windows.1 = f32[3,1,8,256]{3,2,1,0:T(8,128)} custom-call(f32[32,4,128]{2,1,0:T(4,128)S(1)} %all_to_all.11.in_ref), custom_call_target="tpu_custom_call" | custom-call | tf_op jit(solution)/shard_map/collect_windows/pallas_call | solution.py:574

commit v8 on v7

--- a/solution.py
+++ b/solution.py
@@ -192,7 +192,7 @@
             whole = whole + weight
         factor_rows.append(packet_lane([weight / whole for weight in weights]))
 
-    first_depth, lane_first, place_rows, first_half = [], [], [], []
+    first_depth, lane_first, first_half, x_rows, depth_rows = [], [], [], [], []
     for tile in range(tiles):
         first_depth.append(anchor_ref[tile, 0])
         first = bounds_ref[lax.axis_index("cols")] + anchor_ref[tile, 1]
@@ -201,12 +201,13 @@
         first_half.append(first_y // LANES)
         lane_first.append(first_y - first_half[tile] * LANES)
         at_x = first_x + (y_ids < first_y).astype(jnp.int32)
-        place_rows.append((at_x * devices + first_depth[tile]).astype(jnp.float32))
+        x_rows.append(at_x.astype(jnp.float32))
+        depth_rows.append(jnp.full((1, rows_y), first_depth[tile], jnp.int32).astype(jnp.float32))
     notes = jnp.concatenate(
         [jnp.zeros((3 * width, rows_y), jnp.float32)]
-        + place_rows
-        + factor_rows
-        + [jnp.zeros((devices - 3 * width - tiles - params - 1, rows_y), jnp.float32)],
+        + x_rows
+        + depth_rows
+        + factor_rows,
         axis=0,
     )
     dip = dip_ref[0].astype(jnp.float32)
@@ -260,13 +261,12 @@
     moves = [zero] * rows_x
     for source in range(depth):
         message = in_ref[source]
-        at = [
-            jnp.broadcast_to(message[:, side + tile : side + tile + 1], (width, LANES))
-            for tile in range(tiles)
+        notes = [
+            jnp.broadcast_to(message[:, side + number : side + number + 1], (width, LANES))
+            for number in range(2 * tiles)
         ]
-        at = jnp.where(low, at[0], at[1])
-        at_x = jnp.floor(at * (1.0 / depth))
-        below_first = in_tile < at - at_x * depth
+        at_x = jnp.where(low, notes[0], notes[1])
+        below_first = in_tile < jnp.where(low, notes[2], notes[3])
         stay = jnp.logical_xor(low, below_first)
         at_stay = jnp.where(stay, at_x, -1.0)
         at_move = jnp.where(stay, -1.0, at_x)
@@ -317,7 +317,7 @@
         return [values[band * width : (band + 1) * width] for band in bands]
 
     def factor(lane, q):
-        at = side + tiles + lane
+        at = side + 2 * tiles + lane
         return jnp.broadcast_to(in_ref[0, q : q + 1, at : at + 1], (width, LANES))
 
     strengths = [factor(0, q) for q in range(params)]
@@ -516,7 +516,7 @@
         and tiles == 2
         and tiles * tile_depth == depth
         and (params + 1) * depth == LANES
-        and 3 * SUBLANES + tiles + params + 1 <= depth
+        and 3 * SUBLANES + 2 * tiles + params + 1 == depth
         and rays % RAY_CHUNKS == 0
         and rows_x * params * (SUBLANES + 2 * PASSES) <= 4 * LANES
     )

time: 28.5 us -> 28.6 us (level)
  no operation moved by 1% of the time
where the time goes in v8:
time: 28.6 us; the launch traced here: 28.4 us
  blocking collectives  24.4 us (85%)
  Pallas kernels  3.99 us (14%)
    all_to_all x1, blocking collectives, shards_by_y(): received = lax.all_to_all(sent, ('par', 'cols'), 0, 0)  14.8 us
    all_to_all x1, blocking collectives, shards_by_y(): windows = lax.all_to_all(layers, ('par', 'cols'), 0, 0)  9.54 us
    pallas_call x1, Pallas kernels, shards_by_y(): pl.pallas_call(source_kernel, out_shape=pltpu.VMEM((devices, width, LANES...  1.74 us
    pallas_call x1, Pallas kernels, shards_by_y(): pl.pallas_call(functools.partial(smooth_kernel, params=params, tiles=tile...  1.39 us
    pallas_call x1, Pallas kernels, shards_by_y(): pl.pallas_call(functools.partial(collect_kernel, width=width), out_shape=...  0.86 us

profile of v8, /device:TPU:0, one launch (start us, length us, event | category | flops | bytes accessed | tf_op | source)
XLA Modules:
  0.0 28.4 jit_solution(2154607534816113301)
XLA Ops:
  0.0 1.7 %sum_rays.1 = f32[32,8,128]{2,1,0:T(8,128)S(1)} custom-call(s32[9]{0:T(128)} %bounds_hbm.1, s32[2,2]{1,0:T(2,128)} %anchor_hbm.1, s32[2]{0:T(128)} %picks_hbm.1, bf16[2,64]{1,0:T(2,128)(2,1)} %rmo_hbm.1, bf16[2,64,3,16,128]{4,3,2,1,0:T(8,128)(2,1)} %sens_hbm.1, s32[1,8,256]{2,1,0:T(8,128)} %dip_hbm.1, f32[3]{0:T(128)} %strength_hbm.1, f32[3,3]{1,0:T(4,128)} %couple_hbm.1), custom_call_target="tpu_custom_call" | custom-call | tf_op jit(solution)/shard_map/sum_rays/pallas_call | solution.py:542
  1.8 14.8 %all_to_all.10.in_ref = f32[32,8,128]{2,1,0:T(8,128)S(1)} all-to-all(f32[32,8,128]{2,1,0:T(8,128)S(1)} %sum_rays.1), channel_id=1, replica_groups=mesh['cols'=8,'par'=4] {'par','cols'}, dimensions={0} | all-to-all | bytes 262144 | tf_op jit(solution)/shard_map/all_to_all | solution.py:556
  16.6 1.4 %smooth_block.1 = f32[32,4,128]{2,1,0:T(4,128)S(1)} custom-call(f32[32,8,128]{2,1,0:T(8,128)S(1)} %all_to_all.10.in_ref), custom_call_target="tpu_custom_call" | custom-call | tf_op jit(solution)/shard_map/smooth_block/pallas_call | solution.py:557
  18.0 9.5 %all_to_all.11.in_ref = f32[32,4,128]{2,1,0:T(4,128)S(1)} all-to-all(f32[32,4,128]{2,1,0:T(4,128)S(1)} %smooth_block.1), channel_id=1, replica_groups=mesh['cols'=8,'par'=4] {'par','cols'}, dimensions={0} | all-to-all | bytes 131072 | tf_op jit(solution)/shard_map/all_to_all | solution.py:573
  27.5 0.9 %collect_windows.1 = f32[3,1,8,256]{3,2,1,0:T(8,128)} custom-call(f32[32,4,128]{2,1,0:T(4,128)S(1)} %all_to_all.11.in_ref), custom_call_target="tpu_custom_call" | custom-call | tf_op jit(solution)/shard_map/collect_windows/pallas_call | solution.py:574

commit v9 on v8

--- a/solution.py
+++ b/solution.py
@@ -106,8 +106,14 @@
 RAY_CHUNKS = 2
 
 
+def exchange_order(cols, par):
+    return sorted(range(cols * par), key=lambda i: (i // par % 2, i % par % 2, i % par // 2, i // par // 2))
+
+
 def block_index():
-    return lax.axis_index("par") * lax.axis_size("cols") + lax.axis_index("cols")
+    col, replica = lax.axis_index("cols"), lax.axis_index("par")
+    odd = lax.rem(col, 2) * 2 + lax.rem(replica, 2)
+    return (odd * (lax.axis_size("par") // 2) + replica // 2) * (lax.axis_size("cols") // 2) + col // 2
 
 
 def lane_ids(shape):
@@ -247,7 +253,7 @@
             )
 
 
-def smooth_kernel(in_ref, out_ref, layer_ref, *, params, tiles, replicas, rows_x, rows_y):
+def smooth_kernel(in_ref, out_ref, layer_ref, skip_ref, *, params, tiles, replicas, rows_x, rows_y):
     depth, width, _ = in_ref.shape
     groups = LANES // depth
     halves = rows_x // groups
@@ -255,21 +261,29 @@
     side = rows
     lane = lane_ids((width, LANES))
     low = lane % depth < depth // 2
-    in_tile = (lane % (depth // 2)).astype(jnp.float32)
     zero = jnp.zeros((width, LANES), jnp.float32)
+    all_lanes = lane_ids((depth, LANES))
+    all_low = all_lanes % depth < depth // 2
+    first_z = [
+        jnp.broadcast_to(in_ref[:, 0, side + tiles + tile : side + tiles + tile + 1], (depth, LANES))
+        for tile in range(tiles)
+    ]
+    behind = (all_lanes % (depth // 2)).astype(jnp.float32) < jnp.where(all_low, *first_z)
+    stay = jnp.logical_xor(all_low, behind)
+    out_of_grid = -2.0 * rows_x
+    skip_ref[0] = jnp.where(stay, 0.0, out_of_grid)
+    skip_ref[1] = jnp.where(stay, out_of_grid, 0.0)
     stays = [zero] * rows_x
     moves = [zero] * rows_x
     for source in range(depth):
         message = in_ref[source]
-        notes = [
-            jnp.broadcast_to(message[:, side + number : side + number + 1], (width, LANES))
-            for number in range(2 * tiles)
+        at_x = [
+            jnp.broadcast_to(message[:, side + tile : side + tile + 1], (width, LANES))
+            for tile in range(tiles)
         ]
-        at_x = jnp.where(low, notes[0], notes[1])
-        below_first = in_tile < jnp.where(low, notes[2], notes[3])
-        stay = jnp.logical_xor(low, below_first)
-        at_stay = jnp.where(stay, at_x, -1.0)
-        at_move = jnp.where(stay, -1.0, at_x)
+        at_x = jnp.where(low, *at_x)
+        at_stay = at_x + skip_ref[0, source : source + 1, :]
+        at_move = at_x + skip_ref[1, source : source + 1, :]
         for x in range(rows_x):
             stays[x] = stays[x] + jnp.where(at_stay == float(x), message, 0.0)
             moves[x] = moves[x] + jnp.where(at_move == float(x), message, 0.0)
@@ -290,13 +304,15 @@
                 centre = jnp.where(block == group, roll_lanes(stays[x], shift) + moved, centre)
             current[param].append([None, centre, None])
 
+    run = depth // replicas // 2
+    stride = 2 * replicas
+    order = exchange_order(depth // replicas, replicas)
     dip = []
     for half in range(halves):
-        columns = depth // replicas
         for group in range(groups):
-            for replica in range(replicas):
-                layer_ref[half, pl.ds(group * depth + replica, columns, replicas), :] = in_ref[
-                    replica * columns : (replica + 1) * columns, group * halves + half, :
+            for place in range(0, depth, run):
+                layer_ref[half, pl.ds(group * depth + order[place], run, stride), :] = in_ref[
+                    place : place + run, group * halves + half, :
                 ]
         dip.append(jnp.transpose(layer_ref[half])[:rows])
 
@@ -466,9 +482,9 @@
     pieces.append(jnp.zeros((LANES - used, LANES), jnp.float32))
     layer_ref[0] = jnp.transpose(jnp.concatenate(pieces, axis=0))
     for group in range(groups):
-        for replica in range(replicas):
-            out_ref[replica * columns : (replica + 1) * columns, group, :] = layer_ref[
-                0, pl.ds(group * depth + replica, columns, replicas), :
+        for place in range(0, depth, run):
+            out_ref[place : place + run, group, :] = layer_ref[
+                0, pl.ds(group * depth + order[place], run, stride), :
             ]
 
 
@@ -518,6 +534,8 @@
         and (params + 1) * depth == LANES
         and 3 * SUBLANES + 2 * tiles + params + 1 == depth
         and rays % RAY_CHUNKS == 0
+        and lax.axis_size("cols") % 2 == 0
+        and lax.axis_size("par") % 2 == 0
         and rows_x * params * (SUBLANES + 2 * PASSES) <= 4 * LANES
     )
 
@@ -529,6 +547,7 @@
     _, rows_x, rows_y = dip_class.shape
     replicas = lax.axis_size("par")
     devices = lax.axis_size("cols") * replicas
+    exchange = [exchange_order(devices // replicas, replicas)]
     width = rows_y // devices
     groups = LANES // devices
     hbm = pl.BlockSpec(memory_space=pltpu.HBM)
@@ -553,7 +572,7 @@
         compiler_params=pltpu.CompilerParams(vmem_limit_bytes=32 << 20),
         name="sum_rays",
     )(*(pltpu.with_memory_space_constraint(array, pltpu.HBM) for array in arguments))
-    received = lax.all_to_all(sent, ("par", "cols"), 0, 0)
+    received = lax.all_to_all(sent, ("cols", "par"), 0, 0, axis_index_groups=exchange)
     layers = pl.pallas_call(
         functools.partial(
             smooth_kernel,
@@ -566,11 +585,14 @@
         out_shape=jax.ShapeDtypeStruct((devices, groups, LANES), jnp.float32),
         in_specs=[vmem],
         out_specs=vmem,
-        scratch_shapes=[pltpu.VMEM((rows_x // groups, LANES, LANES), jnp.float32)],
+        scratch_shapes=[
+            pltpu.VMEM((rows_x // groups, LANES, LANES), jnp.float32),
+            pltpu.VMEM((2, devices, LANES), jnp.float32),
+        ],
         compiler_params=pltpu.CompilerParams(vmem_limit_bytes=32 << 20),
         name="smooth_block",
     )(received)
-    windows = lax.all_to_all(layers, ("par", "cols"), 0, 0)
+    windows = lax.all_to_all(layers, ("cols", "par"), 0, 0, axis_index_groups=exchange)
     return pl.pallas_call(
         functools.partial(collect_kernel, width=width),
         out_shape=jax.ShapeDtypeStruct((params, 1, rows_x, rows_y), jnp.float32),

time: 28.6 us -> 28.5 us (level)
  no operation moved by 1% of the time
where the time goes in v9:
time: 28.5 us; the launch traced here: 28.3 us
  blocking collectives  24.3 us (85%)
  Pallas kernels  4.01 us (14%)
    all_to_all x1, blocking collectives, shards_by_y(): lax.all_to_all(sent, ('cols', 'par'), 0, 0, axis_index_groups=exchange)  14.8 us
    all_to_all x1, blocking collectives, shards_by_y(): lax.all_to_all(layers, ('cols', 'par'), 0, 0, axis_index_groups=exchange)  9.41 us
    pallas_call x1, Pallas kernels, shards_by_y(): pl.pallas_call(source_kernel, out_shape=pltpu.VMEM((devices, width, LANES...  1.74 us
    pallas_call x1, Pallas kernels, shards_by_y(): pl.pallas_call(functools.partial(smooth_kernel, params=params, tiles=tile...  1.4 us
    pallas_call x1, Pallas kernels, shards_by_y(): pl.pallas_call(functools.partial(collect_kernel, width=width), out_shape=...  0.86 us

profile of v9, /device:TPU:0, one launch (start us, length us, event | category | flops | bytes accessed | tf_op | source)
XLA Modules:
  0.0 28.3 jit_solution(4693225516446606977)
XLA Ops:
  0.0 1.7 %sum_rays.1 = f32[32,8,128]{2,1,0:T(8,128)S(1)} custom-call(s32[9]{0:T(128)} %bounds_hbm.1, s32[2,2]{1,0:T(2,128)} %anchor_hbm.1, s32[2]{0:T(128)} %picks_hbm.1, bf16[2,64]{1,0:T(2,128)(2,1)} %rmo_hbm.1, bf16[2,64,3,16,128]{4,3,2,1,0:T(8,128)(2,1)} %sens_hbm.1, s32[1,8,256]{2,1,0:T(8,128)} %dip_hbm.1, f32[3]{0:T(128)} %strength_hbm.1, f32[3,3]{1,0:T(4,128)} %couple_hbm.1), custom_call_target="tpu_custom_call" | custom-call | tf_op jit(solution)/shard_map/sum_rays/pallas_call | solution.py:561
  1.8 14.8 %all_to_all.10.in_ref = f32[32,8,128]{2,1,0:T(8,128)S(1)} all-to-all(f32[32,8,128]{2,1,0:T(8,128)S(1)} %sum_rays.1), channel_id=1, replica_groups={{0,8,16,24,2,10,18,26,1,9,17,25,3,11,19,27,4,12,20,28,6,14,22,30,5,13,2..., dimensions={0} | all-to-all | bytes 262144 | tf_op jit(solution)/shard_map/all_to_all | solution.py:575
  16.6 1.4 %smooth_block.1 = f32[32,4,128]{2,1,0:T(4,128)S(1)} custom-call(f32[32,8,128]{2,1,0:T(8,128)S(1)} %all_to_all.10.in_ref), custom_call_target="tpu_custom_call" | custom-call | tf_op jit(solution)/shard_map/smooth_block/pallas_call | solution.py:576
  18.0 9.4 %all_to_all.11.in_ref = f32[32,4,128]{2,1,0:T(4,128)S(1)} all-to-all(f32[32,4,128]{2,1,0:T(4,128)S(1)} %smooth_block.1), channel_id=1, replica_groups={{0,8,16,24,2,10,18,26,1,9,17,25,3,11,19,27,4,12,20,28,6,14,22,30,5,13,2..., dimensions={0} | all-to-all | bytes 131072 | tf_op jit(solution)/shard_map/all_to_all | solution.py:595
  27.4 0.9 %collect_windows.1 = f32[3,1,8,256]{3,2,1,0:T(8,128)} custom-call(f32[32,4,128]{2,1,0:T(4,128)S(1)} %all_to_all.11.in_ref), custom_call_target="tpu_custom_call" | custom-call | tf_op jit(solution)/shard_map/collect_windows/pallas_call | solution.py:596

commit v10 on v9

--- a/solution.py
+++ b/solution.py
@@ -253,7 +253,7 @@
             )
 
 
-def smooth_kernel(in_ref, out_ref, layer_ref, skip_ref, *, params, tiles, replicas, rows_x, rows_y):
+def smooth_kernel(in_ref, out_ref, layer_ref, *, params, tiles, replicas, rows_x, rows_y):
     depth, width, _ = in_ref.shape
     groups = LANES // depth
     halves = rows_x // groups
@@ -261,29 +261,29 @@
     side = rows
     lane = lane_ids((width, LANES))
     low = lane % depth < depth // 2
+    in_tile = (lane % (depth // 2)).astype(jnp.float32)
     zero = jnp.zeros((width, LANES), jnp.float32)
-    all_lanes = lane_ids((depth, LANES))
-    all_low = all_lanes % depth < depth // 2
-    first_z = [
-        jnp.broadcast_to(in_ref[:, 0, side + tiles + tile : side + tiles + tile + 1], (depth, LANES))
-        for tile in range(tiles)
-    ]
-    behind = (all_lanes % (depth // 2)).astype(jnp.float32) < jnp.where(all_low, *first_z)
-    stay = jnp.logical_xor(all_low, behind)
-    out_of_grid = -2.0 * rows_x
-    skip_ref[0] = jnp.where(stay, 0.0, out_of_grid)
-    skip_ref[1] = jnp.where(stay, out_of_grid, 0.0)
     stays = [zero] * rows_x
     moves = [zero] * rows_x
+    from_lane = lax.broadcasted_iota(jnp.int32, (LANES, 2 * LANES), 0)
+    to_lane = lane_ids((LANES, 2 * LANES))
+    tile_of = (to_lane % depth) // (depth // 2)
+    spread = from_lane == side + tile_of + jnp.where(to_lane < LANES, 0, tiles)
+    packets = in_ref[...].reshape(depth * width, LANES)
+    packet_lanes = lane_ids(packets.shape)
+    is_note = jnp.logical_and(packet_lanes >= side, packet_lanes < side + 2 * tiles)
+    notes = jnp.dot(
+        jnp.where(is_note, packets, 0.0).astype(jnp.bfloat16),
+        jnp.where(spread, 1.0, 0.0).astype(jnp.bfloat16),
+        preferred_element_type=jnp.float32,
+    )
     for source in range(depth):
         message = in_ref[source]
-        at_x = [
-            jnp.broadcast_to(message[:, side + tile : side + tile + 1], (width, LANES))
-            for tile in range(tiles)
-        ]
-        at_x = jnp.where(low, *at_x)
-        at_stay = at_x + skip_ref[0, source : source + 1, :]
-        at_move = at_x + skip_ref[1, source : source + 1, :]
+        at_x = notes[source * width : (source + 1) * width, :LANES]
+        below_first = in_tile < notes[source * width : (source + 1) * width, LANES:]
+        stay = jnp.logical_xor(low, below_first)
+        at_stay = jnp.where(stay, at_x, -1.0)
+        at_move = jnp.where(stay, -1.0, at_x)
         for x in range(rows_x):
             stays[x] = stays[x] + jnp.where(at_stay == float(x), message, 0.0)
             moves[x] = moves[x] + jnp.where(at_move == float(x), message, 0.0)
@@ -585,10 +585,7 @@
         out_shape=jax.ShapeDtypeStruct((devices, groups, LANES), jnp.float32),
         in_specs=[vmem],
         out_specs=vmem,
-        scratch_shapes=[
-            pltpu.VMEM((rows_x // groups, LANES, LANES), jnp.float32),
-            pltpu.VMEM((2, devices, LANES), jnp.float32),
-        ],
+        scratch_shapes=[pltpu.VMEM((rows_x // groups, LANES, LANES), jnp.float32)],
         compiler_params=pltpu.CompilerParams(vmem_limit_bytes=32 << 20),
         name="smooth_block",
     )(received)

time: 28.5 us -> 28.4 us (level)
  no operation moved by 1% of the time
where the time goes in v10:
time: 28.4 us; the launch traced here: 28.2 us
  blocking collectives  24.3 us (86%)
  Pallas kernels  3.95 us (14%)
    all_to_all x1, blocking collectives, shards_by_y(): lax.all_to_all(sent, ('cols', 'par'), 0, 0, axis_index_groups=exchange)  14.8 us
    all_to_all x1, blocking collectives, shards_by_y(): lax.all_to_all(layers, ('cols', 'par'), 0, 0, axis_index_groups=exchange)  9.41 us
    pallas_call x1, Pallas kernels, shards_by_y(): pl.pallas_call(source_kernel, out_shape=pltpu.VMEM((devices, width, LANES...  1.74 us
    pallas_call x1, Pallas kernels, shards_by_y(): pl.pallas_call(functools.partial(smooth_kernel, params=params, tiles=tile...  1.35 us
    pallas_call x1, Pallas kernels, shards_by_y(): pl.pallas_call(functools.partial(collect_kernel, width=width), out_shape=...  0.86 us

profile of v10, /device:TPU:0, one launch (start us, length us, event | category | flops | bytes accessed | tf_op | source)
XLA Modules:
  0.0 28.2 jit_solution(3326327569728901665)
XLA Ops:
  0.0 1.7 %sum_rays.1 = f32[32,8,128]{2,1,0:T(8,128)S(1)} custom-call(s32[9]{0:T(128)} %bounds_hbm.1, s32[2,2]{1,0:T(2,128)} %anchor_hbm.1, s32[2]{0:T(128)} %picks_hbm.1, bf16[2,64]{1,0:T(2,128)(2,1)} %rmo_hbm.1, bf16[2,64,3,16,128]{4,3,2,1,0:T(8,128)(2,1)} %sens_hbm.1, s32[1,8,256]{2,1,0:T(8,128)} %dip_hbm.1, f32[3]{0:T(128)} %strength_hbm.1, f32[3,3]{1,0:T(4,128)} %couple_hbm.1), custom_call_target="tpu_custom_call" | custom-call | tf_op jit(solution)/shard_map/sum_rays/pallas_call | solution.py:561
  1.8 14.8 %all_to_all.10.in_ref = f32[32,8,128]{2,1,0:T(8,128)S(1)} all-to-all(f32[32,8,128]{2,1,0:T(8,128)S(1)} %sum_rays.1), channel_id=1, replica_groups={{0,8,16,24,2,10,18,26,1,9,17,25,3,11,19,27,4,12,20,28,6,14,22,30,5,13,2..., dimensions={0} | all-to-all | bytes 262144 | tf_op jit(solution)/shard_map/all_to_all | solution.py:575
  16.6 1.4 %smooth_block.1 = f32[32,4,128]{2,1,0:T(4,128)S(1)} custom-call(f32[32,8,128]{2,1,0:T(8,128)S(1)} %all_to_all.10.in_ref), custom_call_target="tpu_custom_call" | custom-call | tf_op jit(solution)/shard_map/smooth_block/pallas_call | solution.py:576
  18.0 9.4 %all_to_all.11.in_ref = f32[32,4,128]{2,1,0:T(4,128)S(1)} all-to-all(f32[32,4,128]{2,1,0:T(4,128)S(1)} %smooth_block.1), channel_id=1, replica_groups={{0,8,16,24,2,10,18,26,1,9,17,25,3,11,19,27,4,12,20,28,6,14,22,30,5,13,2..., dimensions={0} | all-to-all | bytes 131072 | tf_op jit(solution)/shard_map/all_to_all | solution.py:592
  27.4 0.9 %collect_windows.1 = f32[3,1,8,256]{3,2,1,0:T(8,128)} custom-call(f32[32,4,128]{2,1,0:T(4,128)S(1)} %all_to_all.11.in_ref), custom_call_target="tpu_custom_call" | custom-call | tf_op jit(solution)/shard_map/collect_windows/pallas_call | solution.py:593

commit v11 on v10

--- a/solution.py
+++ b/solution.py
@@ -190,30 +190,38 @@
             lane = jnp.where(place_in_packet == q, value, lane)
         return lane
 
-    factor_rows = [packet_lane([strength_ref[q] for q in range(params)])]
+    factors = [jnp.full((1, rows_y), strength_ref[q], jnp.float32) for q in range(params)]
     for p in range(params):
         weights = [jnp.full((1, rows_y), couple_ref[p, q], jnp.float32) for q in range(params)]
         whole = weights[0]
         for weight in weights[1:]:
             whole = whole + weight
-        factor_rows.append(packet_lane([weight / whole for weight in weights]))
-
+        factors.extend(weight / whole for weight in weights)
+
+    factor_rows = [
+        packet_lane(factors[first : first + 2 * params]) for first in range(0, len(factors), 2 * params)
+    ]
+    column_first = bounds_ref[lax.axis_index("cols")]
+    column_x = column_first // rows_y
+    from_x = column_x + (y_ids < column_first - column_x * rows_y).astype(jnp.int32)
     first_depth, lane_first, first_half, x_rows, depth_rows = [], [], [], [], []
     for tile in range(tiles):
         first_depth.append(anchor_ref[tile, 0])
-        first = bounds_ref[lax.axis_index("cols")] + anchor_ref[tile, 1]
+        first = column_first + anchor_ref[tile, 1]
         first_x = first // rows_y
         first_y = first - first_x * rows_y
         first_half.append(first_y // LANES)
         lane_first.append(first_y - first_half[tile] * LANES)
         at_x = first_x + (y_ids < first_y).astype(jnp.int32)
-        x_rows.append(at_x.astype(jnp.float32))
+        x_rows.append((at_x - from_x).astype(jnp.float32))
         depth_rows.append(jnp.full((1, rows_y), first_depth[tile], jnp.int32).astype(jnp.float32))
     notes = jnp.concatenate(
         [jnp.zeros((3 * width, rows_y), jnp.float32)]
         + x_rows
         + depth_rows
-        + factor_rows,
+        + [from_x.astype(jnp.float32)]
+        + factor_rows
+        + [jnp.zeros((devices - 3 * width - 2 * tiles - 1 - len(factor_rows), rows_y), jnp.float32)],
         axis=0,
     )
     dip = dip_ref[0].astype(jnp.float32)
@@ -265,28 +273,41 @@
     zero = jnp.zeros((width, LANES), jnp.float32)
     stays = [zero] * rows_x
     moves = [zero] * rows_x
-    from_lane = lax.broadcasted_iota(jnp.int32, (LANES, 2 * LANES), 0)
-    to_lane = lane_ids((LANES, 2 * LANES))
+    from_lane = lax.broadcasted_iota(jnp.int32, (LANES, 3 * LANES), 0)
+    to_lane = lane_ids((LANES, 3 * LANES))
     tile_of = (to_lane % depth) // (depth // 2)
-    spread = from_lane == side + tile_of + jnp.where(to_lane < LANES, 0, tiles)
+    spread = from_lane == side + jnp.where(
+        to_lane < 2 * LANES, tile_of + jnp.where(to_lane < LANES, 0, tiles), 2 * tiles
+    )
     packets = in_ref[...].reshape(depth * width, LANES)
     packet_lanes = lane_ids(packets.shape)
-    is_note = jnp.logical_and(packet_lanes >= side, packet_lanes < side + 2 * tiles)
+    is_note = jnp.logical_and(packet_lanes >= side, packet_lanes <= side + 2 * tiles)
     notes = jnp.dot(
         jnp.where(is_note, packets, 0.0).astype(jnp.bfloat16),
         jnp.where(spread, 1.0, 0.0).astype(jnp.bfloat16),
         preferred_element_type=jnp.float32,
     )
-    for source in range(depth):
-        message = in_ref[source]
-        at_x = notes[source * width : (source + 1) * width, :LANES]
-        below_first = in_tile < notes[source * width : (source + 1) * width, LANES:]
-        stay = jnp.logical_xor(low, below_first)
-        at_stay = jnp.where(stay, at_x, -1.0)
-        at_move = jnp.where(stay, -1.0, at_x)
+    columns = depth // replicas
+    places = {device: place for place, device in enumerate(exchange_order(columns, replicas))}
+    for column in range(columns):
+        near = [[zero, zero], [zero, zero]]
+        for replica in range(replicas):
+            place = places[column * replicas + replica]
+            message = in_ref[place]
+            rows_of = slice(place * width, (place + 1) * width)
+            second = notes[rows_of, :LANES] > 0.5
+            stay = jnp.logical_xor(low, in_tile < notes[rows_of, LANES : 2 * LANES])
+            for sums, values in zip(near, (jnp.where(stay, message, 0.0), jnp.where(stay, 0.0, message))):
+                sums[0] = sums[0] + jnp.where(second, 0.0, values)
+                sums[1] = sums[1] + jnp.where(second, values, 0.0)
+        from_x = notes[rows_of, 2 * LANES :]
         for x in range(rows_x):
-            stays[x] = stays[x] + jnp.where(at_stay == float(x), message, 0.0)
-            moves[x] = moves[x] + jnp.where(at_move == float(x), message, 0.0)
+            here = from_x == float(x)
+            for field, sums in zip((stays, moves), near):
+                field[x] = field[x] + jnp.where(here, sums[0], 0.0)
+                if x + 1 < rows_x:
+                    field[x + 1] = field[x + 1] + jnp.where(here, sums[1], 0.0)
+
     block = lane // depth
     current = []
     for param in range(params):
@@ -333,8 +354,10 @@
         return [values[band * width : (band + 1) * width] for band in bands]
 
     def factor(lane, q):
-        at = side + 2 * tiles + lane
-        return jnp.broadcast_to(in_ref[0, q : q + 1, at : at + 1], (width, LANES))
+        number = lane * params + q
+        at = side + 2 * tiles + 1 + number // (2 * params)
+        row = number % (2 * params)
+        return jnp.broadcast_to(in_ref[0, row : row + 1, at : at + 1], (width, LANES))
 
     strengths = [factor(0, q) for q in range(params)]
     keeps = [1.0 / strength - 4.0 for strength in strengths]
@@ -532,7 +555,9 @@
         and tiles == 2
         and tiles * tile_depth == depth
         and (params + 1) * depth == LANES
-        and 3 * SUBLANES + 2 * tiles + params + 1 == depth
+        and 2 * params <= SUBLANES
+        and 3 * SUBLANES + 2 * tiles + 1 + (params + 2) // 2 < depth
+        and CAP <= 2 * rows_y
         and rays % RAY_CHUNKS == 0
         and lax.axis_size("cols") % 2 == 0
         and lax.axis_size("par") % 2 == 0

time: 28.4 us -> 28.4 us (level)
  no operation moved by 1% of the time
where the time goes in v11:
time: 28.4 us; the launch traced here: 28.2 us
  blocking collectives  24.3 us (86%)
  Pallas kernels  3.88 us (14%)
    all_to_all x1, blocking collectives, shards_by_y(): lax.all_to_all(sent, ('cols', 'par'), 0, 0, axis_index_groups=exchange)  14.8 us
    all_to_all x1, blocking collectives, shards_by_y(): lax.all_to_all(layers, ('cols', 'par'), 0, 0, axis_index_groups=exchange)  9.41 us
    pallas_call x1, Pallas kernels, shards_by_y(): pl.pallas_call(source_kernel, out_shape=pltpu.VMEM((devices, width, LANES...  1.74 us
    pallas_call x1, Pallas kernels, shards_by_y(): pl.pallas_call(functools.partial(smooth_kernel, params=params, tiles=tile...  1.27 us
    pallas_call x1, Pallas kernels, shards_by_y(): pl.pallas_call(functools.partial(collect_kernel, width=width), out_shape=...  0.86 us

profile of v11, /device:TPU:0, one launch (start us, length us, event | category | flops | bytes accessed | tf_op | source)
XLA Modules:
  0.0 28.2 jit_solution(16104420552497926659)
XLA Ops:
  0.0 1.7 %sum_rays.1 = f32[32,8,128]{2,1,0:T(8,128)S(1)} custom-call(s32[9]{0:T(128)} %bounds_hbm.1, s32[2,2]{1,0:T(2,128)} %anchor_hbm.1, s32[2]{0:T(128)} %picks_hbm.1, bf16[2,64]{1,0:T(2,128)(2,1)} %rmo_hbm.1, bf16[2,64,3,16,128]{4,3,2,1,0:T(8,128)(2,1)} %sens_hbm.1, s32[1,8,256]{2,1,0:T(8,128)} %dip_hbm.1, f32[3]{0:T(128)} %strength_hbm.1, f32[3,3]{1,0:T(4,128)} %couple_hbm.1), custom_call_target="tpu_custom_call" | custom-call | tf_op jit(solution)/shard_map/sum_rays/pallas_call | solution.py:586
  1.8 14.8 %all_to_all.10.in_ref = f32[32,8,128]{2,1,0:T(8,128)S(1)} all-to-all(f32[32,8,128]{2,1,0:T(8,128)S(1)} %sum_rays.1), channel_id=1, replica_groups={{0,8,16,24,2,10,18,26,1,9,17,25,3,11,19,27,4,12,20,28,6,14,22,30,5,13,2..., dimensions={0} | all-to-all | bytes 262144 | tf_op jit(solution)/shard_map/all_to_all | solution.py:600
  16.6 1.3 %smooth_block.1 = f32[32,4,128]{2,1,0:T(4,128)S(1)} custom-call(f32[32,8,128]{2,1,0:T(8,128)S(1)} %all_to_all.10.in_ref), custom_call_target="tpu_custom_call" | custom-call | tf_op jit(solution)/shard_map/smooth_block/pallas_call | solution.py:601
  17.9 9.4 %all_to_all.11.in_ref = f32[32,4,128]{2,1,0:T(4,128)S(1)} all-to-all(f32[32,4,128]{2,1,0:T(4,128)S(1)} %smooth_block.1), channel_id=1, replica_groups={{0,8,16,24,2,10,18,26,1,9,17,25,3,11,19,27,4,12,20,28,6,14,22,30,5,13,2..., dimensions={0} | all-to-all | bytes 131072 | tf_op jit(solution)/shard_map/all_to_all | solution.py:617
  27.3 0.9 %collect_windows.1 = f32[3,1,8,256]{3,2,1,0:T(8,128)} custom-call(f32[32,4,128]{2,1,0:T(4,128)S(1)} %all_to_all.11.in_ref), custom_call_target="tpu_custom_call" | custom-call | tf_op jit(solution)/shard_map/collect_windows/pallas_call | solution.py:618

commit v12 on v11

--- a/solution.py
+++ b/solution.py
@@ -271,6 +271,18 @@
     low = lane % depth < depth // 2
     in_tile = (lane % (depth // 2)).astype(jnp.float32)
     zero = jnp.zeros((width, LANES), jnp.float32)
+    run = depth // replicas // 2
+    stride = 2 * replicas
+    order = exchange_order(depth // replicas, replicas)
+    dip = []
+    for half in range(halves):
+        for group in range(groups):
+            for place in range(0, depth, run):
+                layer_ref[half, pl.ds(group * depth + order[place], run, stride), :] = in_ref[
+                    place : place + run, group * halves + half, :
+                ]
+        dip.append(jnp.transpose(layer_ref[half])[:rows])
+
     stays = [zero] * rows_x
     moves = [zero] * rows_x
     from_lane = lax.broadcasted_iota(jnp.int32, (LANES, 3 * LANES), 0)
@@ -324,18 +336,6 @@
                 )
                 centre = jnp.where(block == group, roll_lanes(stays[x], shift) + moved, centre)
             current[param].append([None, centre, None])
-
-    run = depth // replicas // 2
-    stride = 2 * replicas
-    order = exchange_order(depth // replicas, replicas)
-    dip = []
-    for half in range(halves):
-        for group in range(groups):
-            for place in range(0, depth, run):
-                layer_ref[half, pl.ds(group * depth + order[place], run, stride), :] = in_ref[
-                    place : place + run, group * halves + half, :
-                ]
-        dip.append(jnp.transpose(layer_ref[half])[:rows])
 
     lanes = lane_ids((rows, LANES))
     z = lanes % depth

time: 28.4 us -> 28.3 us (level)
  no operation moved by 1% of the time
where the time goes in v12:
time: 28.3 us; the launch traced here: 28.1 us
  blocking collectives  24.3 us (86%)
  Pallas kernels  3.88 us (14%)
    all_to_all x1, blocking collectives, shards_by_y(): lax.all_to_all(sent, ('cols', 'par'), 0, 0, axis_index_groups=exchange)  14.8 us
    all_to_all x1, blocking collectives, shards_by_y(): lax.all_to_all(layers, ('cols', 'par'), 0, 0, axis_index_groups=exchange)  9.41 us
    pallas_call x1, Pallas kernels, shards_by_y(): pl.pallas_call(source_kernel, out_shape=pltpu.VMEM((devices, width, LANES...  1.74 us
    pallas_call x1, Pallas kernels, shards_by_y(): pl.pallas_call(functools.partial(smooth_kernel, params=params, tiles=tile...  1.27 us
    pallas_call x1, Pallas kernels, shards_by_y(): pl.pallas_call(functools.partial(collect_kernel, width=width), out_shape=...  0.86 us

profile of v12, /device:TPU:0, one launch (start us, length us, event | category | flops | bytes accessed | tf_op | source)
XLA Modules:
  0.0 28.1 jit_solution(2230103896469130131)
XLA Ops:
  0.0 1.7 %sum_rays.1 = f32[32,8,128]{2,1,0:T(8,128)S(1)} custom-call(s32[9]{0:T(128)} %bounds_hbm.1, s32[2,2]{1,0:T(2,128)} %anchor_hbm.1, s32[2]{0:T(128)} %picks_hbm.1, bf16[2,64]{1,0:T(2,128)(2,1)} %rmo_hbm.1, bf16[2,64,3,16,128]{4,3,2,1,0:T(8,128)(2,1)} %sens_hbm.1, s32[1,8,256]{2,1,0:T(8,128)} %dip_hbm.1, f32[3]{0:T(128)} %strength_hbm.1, f32[3,3]{1,0:T(4,128)} %couple_hbm.1), custom_call_target="tpu_custom_call" | custom-call | tf_op jit(solution)/shard_map/sum_rays/pallas_call | solution.py:586
  1.8 14.8 %all_to_all.10.in_ref = f32[32,8,128]{2,1,0:T(8,128)S(1)} all-to-all(f32[32,8,128]{2,1,0:T(8,128)S(1)} %sum_rays.1), channel_id=1, replica_groups={{0,8,16,24,2,10,18,26,1,9,17,25,3,11,19,27,4,12,20,28,6,14,22,30,5,13,2..., dimensions={0} | all-to-all | bytes 262144 | tf_op jit(solution)/shard_map/all_to_all | solution.py:600
  16.6 1.3 %smooth_block.1 = f32[32,4,128]{2,1,0:T(4,128)S(1)} custom-call(f32[32,8,128]{2,1,0:T(8,128)S(1)} %all_to_all.10.in_ref), custom_call_target="tpu_custom_call" | custom-call | tf_op jit(solution)/shard_map/smooth_block/pallas_call | solution.py:601
  17.9 9.4 %all_to_all.11.in_ref = f32[32,4,128]{2,1,0:T(4,128)S(1)} all-to-all(f32[32,4,128]{2,1,0:T(4,128)S(1)} %smooth_block.1), channel_id=1, replica_groups={{0,8,16,24,2,10,18,26,1,9,17,25,3,11,19,27,4,12,20,28,6,14,22,30,5,13,2..., dimensions={0} | all-to-all | bytes 131072 | tf_op jit(solution)/shard_map/all_to_all | solution.py:617
  27.3 0.9 %collect_windows.1 = f32[3,1,8,256]{3,2,1,0:T(8,128)} custom-call(f32[32,4,128]{2,1,0:T(4,128)S(1)} %all_to_all.11.in_ref), custom_call_target="tpu_custom_call" | custom-call | tf_op jit(solution)/shard_map/collect_windows/pallas_call | solution.py:618

commit v13 on v12

--- a/solution.py
+++ b/solution.py
@@ -181,30 +181,28 @@
         column = jnp.sum(jnp.where(diagonal, weight, 0.0), axis=1, keepdims=True)
         weight_ref[tile] = jnp.broadcast_to(column, (rays, LANES))
 
-    y_ids = lane_ids((1, rows_y))
-    place_in_packet = lax.rem(y_ids, width)
-
-    def packet_lane(values):
-        lane = jnp.zeros((1, rows_y), jnp.float32)
-        for q, value in enumerate(values):
-            lane = jnp.where(place_in_packet == q, value, lane)
-        return lane
-
-    factors = [jnp.full((1, rows_y), strength_ref[q], jnp.float32) for q in range(params)]
+    side = 3 * width
+    lane = lane_ids((width, LANES))
+    row = lax.broadcasted_iota(jnp.int32, (width, LANES), 0)
+    factors = [jnp.full((width, LANES), strength_ref[q], jnp.float32) for q in range(params)]
     for p in range(params):
-        weights = [jnp.full((1, rows_y), couple_ref[p, q], jnp.float32) for q in range(params)]
+        weights = [jnp.full((width, LANES), couple_ref[p, q], jnp.float32) for q in range(params)]
         whole = weights[0]
         for weight in weights[1:]:
             whole = whole + weight
         factors.extend(weight / whole for weight in weights)
-
-    factor_rows = [
-        packet_lane(factors[first : first + 2 * params]) for first in range(0, len(factors), 2 * params)
-    ]
+    note = jnp.zeros((width, LANES), jnp.float32)
+    for number, factor in enumerate(factors):
+        at = side + 2 * tiles + 1 + number // (2 * params)
+        note = jnp.where(jnp.logical_and(lane == at, row == number % (2 * params)), factor, note)
+
     column_first = bounds_ref[lax.axis_index("cols")]
     column_x = column_first // rows_y
-    from_x = column_x + (y_ids < column_first - column_x * rows_y).astype(jnp.int32)
-    first_depth, lane_first, first_half, x_rows, depth_rows = [], [], [], [], []
+    column_y = column_first - column_x * rows_y
+    first_depth, lane_first, first_half = [], [], []
+    whole_note = jnp.where(lane == side + 2 * tiles, column_x, 0)
+    more_below = jnp.where(lane == side + 2 * tiles, column_y, 0)
+    less_below = jnp.zeros((width, LANES), jnp.int32)
     for tile in range(tiles):
         first_depth.append(anchor_ref[tile, 0])
         first = column_first + anchor_ref[tile, 1]
@@ -212,24 +210,29 @@
         first_y = first - first_x * rows_y
         first_half.append(first_y // LANES)
         lane_first.append(first_y - first_half[tile] * LANES)
-        at_x = first_x + (y_ids < first_y).astype(jnp.int32)
-        x_rows.append((at_x - from_x).astype(jnp.float32))
-        depth_rows.append(jnp.full((1, rows_y), first_depth[tile], jnp.int32).astype(jnp.float32))
-    notes = jnp.concatenate(
-        [jnp.zeros((3 * width, rows_y), jnp.float32)]
-        + x_rows
-        + depth_rows
-        + [from_x.astype(jnp.float32)]
-        + factor_rows
-        + [jnp.zeros((devices - 3 * width - 2 * tiles - 1 - len(factor_rows), rows_y), jnp.float32)],
-        axis=0,
-    )
+        whole_note = jnp.where(lane == side + tile, first_x - column_x, whole_note)
+        whole_note = jnp.where(lane == side + tiles + tile, first_depth[tile], whole_note)
+        more_below = jnp.where(lane == side + tile, first_y, more_below)
+        less_below = jnp.where(lane == side + tile, column_y, less_below)
+    note = note + whole_note.astype(jnp.float32)
     dip = dip_ref[0].astype(jnp.float32)
     count = LANES // width
+    in_window = lane < side
     for device in range(devices):
-        out_ref[device] = roll_lanes(dip, width - device * width)[:, :LANES]
-
-    parts = [[[None] * tiles for _ in range(params)] for _ in range(halves)]
+        y = row + device * width
+        steps = jnp.where(y < more_below, 1.0, 0.0) - jnp.where(y < less_below, 1.0, 0.0)
+        window = roll_lanes(dip, width - device * width)[:, :LANES]
+        out_ref[device] = jnp.where(in_window, window, note + steps)
+
+    row_ids = lax.broadcasted_iota(jnp.int32, (LANES, LANES), 0)
+    first_tile = lane_ids((LANES, LANES)) % devices < tile_depth
+    half_before = jnp.where(first_tile, first_half[0], first_half[1])
+    half_after = jnp.where(half_before == halves - 1, 0, half_before + 1)
+    half_of = jnp.where(
+        row_ids >= jnp.where(first_tile, lane_first[0], lane_first[1]), half_before, half_after
+    )
+
+    parts = [[None] * tiles for _ in range(params)]
     for tile in range(tiles):
         total = jnp.zeros((params, tile_depth, tile_columns), jnp.float32)
         for ray in range(rays):
@@ -237,28 +240,18 @@
                 large[tile][ray // chunk].wait()
             weight = weight_ref[tile, ray : ray + 1, :]
             total = total + weight[None] * sens_ref[tile, ray].astype(jnp.float32)
-        past = lane_ids((1, LANES)) >= lane_first[tile]
         for param in range(params):
             turned = pltpu.roll(total[param], lax.rem(first_depth[tile], tile_depth), 0)
-            turned = pltpu.roll(turned, lane_first[tile], 1)
-            for half in range(halves):
-                after = lax.rem(first_half[tile] + 1, halves)
-                kept = jnp.logical_or(
-                    jnp.logical_and(past, first_half[tile] == half),
-                    jnp.logical_and(jnp.logical_not(past), after == half),
-                )
-                parts[half][param][tile] = jnp.where(kept, turned, 0.0)
-    in_window = lane_ids((rows_x, LANES)) < 3 * width
+            parts[param][tile] = pltpu.roll(turned, lane_first[tile], 1)
+    rows = [jnp.zeros((devices, tile_columns), jnp.float32)]
+    for param in range(params):
+        rows.extend(parts[param])
+    turned = jnp.transpose(jnp.concatenate(rows, axis=0))
     for half in range(halves):
-        rows = [notes[:, half * LANES : (half + 1) * LANES]]
-        for param in range(params):
-            rows.extend(parts[half][param])
-        turned = jnp.transpose(jnp.concatenate(rows, axis=0))
+        kept = jnp.where(half_of == half, turned, 0.0)
         for place in range(count):
             device = half * count + place
-            out_ref[device] = jnp.where(
-                in_window, out_ref[device], turned[place * width : (place + 1) * width]
-            )
+            out_ref[device] = out_ref[device] + kept[place * width : (place + 1) * width]
 
 
 def smooth_kernel(in_ref, out_ref, layer_ref, *, params, tiles, replicas, rows_x, rows_y):

time: 28.3 us -> 28.4 us (level)
  no operation moved by 1% of the time
where the time goes in v13:
time: 28.4 us; the launch traced here: 28.2 us
  blocking collectives  24.3 us (86%)
  Pallas kernels  3.88 us (14%)
    all_to_all x1, blocking collectives, shards_by_y(): lax.all_to_all(sent, ('cols', 'par'), 0, 0, axis_index_groups=exchange)  14.8 us
    all_to_all x1, blocking collectives, shards_by_y(): lax.all_to_all(layers, ('cols', 'par'), 0, 0, axis_index_groups=exchange)  9.42 us
    pallas_call x1, Pallas kernels, shards_by_y(): pl.pallas_call(source_kernel, out_shape=pltpu.VMEM((devices, width, LANES...  1.74 us
    pallas_call x1, Pallas kernels, shards_by_y(): pl.pallas_call(functools.partial(smooth_kernel, params=params, tiles=tile...  1.27 us
    pallas_call x1, Pallas kernels, shards_by_y(): pl.pallas_call(functools.partial(collect_kernel, width=width), out_shape=...  0.86 us

profile of v13, /device:TPU:0, one launch (start us, length us, event | category | flops | bytes accessed | tf_op | source)
XLA Modules:
  0.0 28.2 jit_solution(18082740100180481516)
XLA Ops:
  0.0 1.7 %sum_rays.1 = f32[32,8,128]{2,1,0:T(8,128)S(1)} custom-call(s32[9]{0:T(128)} %bounds_hbm.1, s32[2,2]{1,0:T(2,128)} %anchor_hbm.1, s32[2]{0:T(128)} %picks_hbm.1, bf16[2,64]{1,0:T(2,128)(2,1)} %rmo_hbm.1, bf16[2,64,3,16,128]{4,3,2,1,0:T(8,128)(2,1)} %sens_hbm.1, s32[1,8,256]{2,1,0:T(8,128)} %dip_hbm.1, f32[3]{0:T(128)} %strength_hbm.1, f32[3,3]{1,0:T(4,128)} %couple_hbm.1), custom_call_target="tpu_custom_call" | custom-call | tf_op jit(solution)/shard_map/sum_rays/pallas_call | solution.py:579
  1.8 14.8 %all_to_all.10.in_ref = f32[32,8,128]{2,1,0:T(8,128)S(1)} all-to-all(f32[32,8,128]{2,1,0:T(8,128)S(1)} %sum_rays.1), channel_id=1, replica_groups={{0,8,16,24,2,10,18,26,1,9,17,25,3,11,19,27,4,12,20,28,6,14,22,30,5,13,2..., dimensions={0} | all-to-all | bytes 262144 | tf_op jit(solution)/shard_map/all_to_all | solution.py:593
  16.6 1.3 %smooth_block.1 = f32[32,4,128]{2,1,0:T(4,128)S(1)} custom-call(f32[32,8,128]{2,1,0:T(8,128)S(1)} %all_to_all.10.in_ref), custom_call_target="tpu_custom_call" | custom-call | tf_op jit(solution)/shard_map/smooth_block/pallas_call | solution.py:594
  17.9 9.4 %all_to_all.11.in_ref = f32[32,4,128]{2,1,0:T(4,128)S(1)} all-to-all(f32[32,4,128]{2,1,0:T(4,128)S(1)} %smooth_block.1), channel_id=1, replica_groups={{0,8,16,24,2,10,18,26,1,9,17,25,3,11,19,27,4,12,20,28,6,14,22,30,5,13,2..., dimensions={0} | all-to-all | bytes 131072 | tf_op jit(solution)/shard_map/all_to_all | solution.py:610
  27.3 0.9 %collect_windows.1 = f32[3,1,8,256]{3,2,1,0:T(8,128)} custom-call(f32[32,4,128]{2,1,0:T(4,128)S(1)} %all_to_all.11.in_ref), custom_call_target="tpu_custom_call" | custom-call | tf_op jit(solution)/shard_map/collect_windows/pallas_call | solution.py:611
